TPU v7x, 512 devices: a whole 4x8x8 slice. The times are simulated.
512 devices in a mesh: dp: 32 (over x, z), pipe: 16 (over y, core).
Axes of the slice: x: 4, y: 8, z: 8, core: 2. Of those that a mesh axis runs over, the one named last changes fastest.
Arguments:
- hidden: bfloat16 [2, 768, 5376], P(None, 'dp', 'pipe'), may hold values from -64 to 64
- norm_gain: float32 [5376], replicated, may hold values from 0.1 to 1.9
- embedding: bfloat16 [131072, 5376], P(('dp', 'pipe')), may hold values from -4 to 4
- targets: int32 [2, 768], P(None, 'dp'), may hold values from 0 to 131071
Outputs:
- token_loss: float32 [2, 768], P(None, 'dp')
All inputs are finite; a program needn't handle non-finite values.
Results may differ from a plain program's by a relative error of at most 0.00054.
Values may be sent and summed in bfloat16 or wider, within the bound.
No kernel may reach another device: no remote copies, remote signals or barrier semaphores. Data moves between devices by JAX's collectives and lax.ppermute only.
A program may use at most 64 MiB of HBM per device.

v0:
```python
import jax
import jax.numpy as jnp
from jax import lax
from jax.sharding import PartitionSpec as P

epsilon = 1e-06


def normalize(rows_in, norm_gain):
    as_float = rows_in.astype(jnp.float32)
    mean_square = jnp.mean(as_float * as_float, axis=-1, keepdims=True)
    return (as_float * lax.rsqrt(mean_square + epsilon) * norm_gain).astype(jnp.bfloat16)


def per_device(hidden, norm_gain, embedding, targets):
    vocab_local = embedding.shape[0]
    sections = lax.axis_size("pipe")
    first_row = (lax.axis_index("dp") * sections + lax.axis_index("pipe")) * vocab_local
    columns = lax.broadcasted_iota(jnp.int32, (1, 1, vocab_local), 2) + first_row
    gathered = lax.all_gather(hidden, "pipe", axis=2, tiled=True)
    piece_rows = lax.all_gather(gathered, "dp", axis=1, tiled=True)
    piece_targets = lax.all_gather(targets, "dp", axis=1, tiled=True)
    normed = normalize(piece_rows, norm_gain)
    logits = jnp.einsum("mrh,vh->mrv", normed, embedding, preferred_element_type=jnp.float32)
    row_peak = jnp.max(logits, axis=2)
    row_total = jnp.sum(jnp.exp(logits - row_peak[:, :, None]), axis=2)
    picked = jnp.sum(jnp.where(piece_targets[:, :, None] == columns, logits, 0.0), axis=2)
    updates = (row_peak, row_total, picked)
    row_peak, row_total, picked = tuple((update for update in updates))
    global_peak = lax.pmax(row_peak, ("dp", "pipe"))
    shifted = row_total * jnp.exp(row_peak - global_peak)
    global_total, global_pick = lax.psum((shifted, picked), ("dp", "pipe"))
    token_loss = global_peak + jnp.log(global_total) - global_pick
    return lax.dynamic_slice_in_dim(
        token_loss, lax.axis_index("dp") * hidden.shape[1], hidden.shape[1], 1
    )


def solution(mesh):
    placed = (P(None, "dp", "pipe"), P(), P(("dp", "pipe"), None), P(None, "dp"))
    return jax.shard_map(
        per_device, mesh=mesh, in_specs=placed, out_specs=P(None, "dp"), check_vma=False
    )
```

profile of v0, /device:TPU:1, one launch (start us, length us, event | category | flops | bytes accessed | tf_op | source)
XLA Modules:
  0.0 406.2 jit_solution(3262085246131679479)
XLA Ops:
  6.5 0.0 copy-start
  6.5 0.0 copy-start.2
  6.5 0.0 all-gather.3.cloned.1.call-start
  6.5 1.1 copy.13
  7.6 33.6 %all_gather.9 = bf16[2,24,5376]{1,0,2:T(2,128)(2,1)} all-gather(bf16[2,24,336]{1,0,2:T(2,128)(2,1)S(1)} %copy.13), channel_id=1, replica_groups=mesh['dp'=32,'pipe'=16] {'pipe'}, dimensions={2}, use_global_device_ids=true | all-gather | bytes 548352 | tf_op jit(solution)/shard_map/all_gather | solution.py:20
  41.2 6.8 %copy.14 = bf16[2,24,5376]{2,0,1:T(2,128)(2,1)} copy(bf16[2,24,5376]{1,0,2:T(2,128)(2,1)} %all_gather.9) | data formatting | bytes 1032192 | tf_op jit(solution)/shard_map/all_gather | solution.py:20
  47.9 0.0 all-gather.3.cloned.1.call-update
  48.0 37.4 %all-gather = s32[32,24,2]{1,2,0:T(2,128)S(1)} all-gather(s32[1,24,2]{1,2,0:T(2,128)} %bitcast.12), channel_id=1, replica_groups=mesh['dp'=32,'pipe'=16] {'dp'}, dimensions={0}, use_global_device_ids=true | all-gather | bytes 6336 | tf_op jit(solution)/shard_map/all_gather | solution.py:22
  85.4 0.1 reshape.17
  85.5 104.4 %all-gather.3.cloned.1.call-done = bf16[2,768,5376]{2,0,1:T(2,128)(2,1)} async-done(((bf16[2,24,5376]{2,0,1:T(2,128)(2,1)}), bf16[2,768,5376]{2,0,1:T(2,128)(2,1)}) %all-gather.3.cloned.1.call-update) | async-done | bytes 16515088 | tf_op jit(solution)/shard_map/all_gather | solution.py:21
  189.9 0.0 copy-start.1
  189.9 9.4 %fusion = f32[2,768]{1,0:T(2,128)S(1)} fusion(bf16[2,768,5376]{2,0,1:T(2,128)(2,1)} %all-gather.3.cloned.1.call-done), kind=kLoop, calls=%fused_computation.2 | loop fusion | flops 24771072 | bytes 16521216 | tf_op jit(solution)/shard_map/reduce_sum | solution.py:11
  199.3 0.0 copy-done
  199.4 0.0 copy-done.2
  199.4 1.3 copy-done.1
  200.7 6.0 %fusion.9 = (f32[2,768]{1,0:T(2,128)S(1)}, f32[2,768,256]{1,2,0:T(8,128)}) fusion(bf16[256,5376]{1,0:T(8,128)(2,1)S(1)} %copy-done, f32[5376]{0:T(1024)S(1)} %copy-done.2, f32[2,768]{1,0:T(2,128)S(1)} %add_rsqrt_fusion, bf16[2,768,5376]{2,0,1:T(2,128)(2,1)S(1)} %copy-done.1), kind=kOutput, calls=%fused_computation.18 | convolution fusion | flops 4261280256 | bytes 20874240 | tf_op jit(solution)/shard_map/mrh,vh->mrv/dot_general | solution.py:24
  206.7 95.8 %pmax.7 = f32[2,768]{1,0:T(2,128)S(1)} all-reduce(f32[2,768]{1,0:T(2,128)S(1)} %get-tuple-element.9), channel_id=1, replica_groups=mesh['dp'=32,'pipe'=16] {'dp','pipe'}, use_global_device_ids=true, to_apply=%region_2.0 | all-reduce | flops 1536 | bytes 12288 | tf_op jit(solution)/shard_map/pmax | solution.py:30
  302.5 1.8 exponential_reduce_fusion
  304.3 94.4 %all-reduce = (f32[2,768]{1,0:T(2,128)S(1)}, f32[2,768]{1,0:T(2,128)S(1)}) all-reduce(f32[2,768]{1,0:T(2,128)S(1)} %get-tuple-element.6, f32[2,768]{1,0:T(2,128)S(1)} %exponential_multiply_fusion), channel_id=1, replica_groups=mesh['dp'=32,'pipe'=16] {'dp','pipe'}, use_global_device_ids=true, to_apply=%region_6.7 | all-reduce | flops 3072 | bytes 24576 | tf_op jit(solution)/shard_map/psum | solution.py:32
  398.7 0.6 dynamic-slice_subtract_fusion
  (4 shorter events, 0.0 us)
Async XLA Ops:
  6.5 192.8 %copy-start = (bf16[256,5376]{1,0:T(8,128)(2,1)S(1)}, bf16[256,5376]{1,0:T(8,128)(2,1)}, u32[]{:S(2)}) copy-start(bf16[256,5376]{1,0:T(8,128)(2,1)} %param.6) | copy-start | bytes 8257540
  6.5 192.8 %copy-start.2 = (f32[5376]{0:T(1024)S(1)}, f32[5376]{0:T(1024)}, u32[]{:S(2)}) copy-start(f32[5376]{0:T(1024)} %param.5) | copy-start | bytes 64516
  6.5 183.3 %all-gather.3.cloned.1.call-start = ((), (), s32[]{:S(2)}) async-start(), calls=%async_computation | async-start | bytes 17031168 | tf_op jit(solution)/shard_map/all_gather | solution.py:21
  189.9 10.8 %copy-start.1 = (bf16[2,768,5376]{2,0,1:T(2,128)(2,1)S(1)}, bf16[2,768,5376]{2,0,1:T(2,128)(2,1)}, u32[]{:S(2)}) copy-start(bf16[2,768,5376]{2,0,1:T(2,128)(2,1)} %all-gather.3.cloned.1.call-done) | copy-start | bytes 49545220
Sparse Core Ops, SparseCore 0:
  48.1 141.7 all-gather.2
where the time goes:
time: 407 us; the launch traced here: 406 us
  blocking collectives  261 us (64%)
  waiting for transfers between devices  104 us (26%)
  between operations  13.5 us (3%)
  other arithmetic  11.9 us (3%)
  local copies, waits for them, and re-layouts  9.26 us (2%)
  matrix products  6.02 us (1%)
    all_gather x1, waiting for transfers between devices, per_device(): piece_rows = lax.all_gather(gathered, 'dp', axis=1, tiled=True)  104 us
    pmax x1, blocking collectives, per_device(): global_peak = lax.pmax(row_peak, ('dp', 'pipe'))  95.8 us
    psum x1, blocking collectives, per_device(): global_total, global_pick = lax.psum((shifted, picked), ('dp', 'pipe'))  94.4 us
    all_gather x1, blocking collectives, per_device(): piece_targets = lax.all_gather(targets, 'dp', axis=1, tiled=True)  37.4 us
    all_gather x1, blocking collectives, per_device(): gathered = lax.all_gather(hidden, 'pipe', axis=2, tiled=True)  33.6 us
    reduce_sum x1, other arithmetic, normalize(): mean_square = jnp.mean(as_float * as_float, axis=-1, keepdims=True)  9.44 us
  transfers between devices with their start and end apart: 1, of which 1 were waited for; matrix products, arithmetic and copies ran while one was open for 0% of the time, Pallas kernels for 0%

commit v1 on v0

v1 whole, which is shorter than its diff:
```python
import jax
import jax.numpy as jnp
import numpy as np
from jax import lax
from jax.experimental import pallas as pl
from jax.experimental.pallas import tpu as pltpu
from jax.sharding import Mesh
from jax.sharding import PartitionSpec as P

epsilon = 1e-06
H = 5376
PART = 672
FULL = 640
REM = PART - FULL
NY = 8
SOURCES = 16
TOKENS = SOURCES * 24
PAIRS = SOURCES // 2
PAIR_ROWS = 256
VOCAB_LOCAL = 256
EARLY = 48
WORDS = 4 * VOCAB_LOCAL
SMALL = pltpu.CompilerParams(vmem_limit_bytes=8 * 1024 * 1024)


def loss_kernel(*refs):
    g_any, blocks = refs[0], refs[1:5]
    gain_ref, target_ref, place_ref, out_ref, g, e, xn, logits, g_sem, e_sem = refs[5:]

    def g_copy(pair):
        rows = pl.ds(pl.multiple_of(pair * PAIR_ROWS, PAIR_ROWS), PAIR_ROWS)
        return pltpu.make_async_copy(g_any.at[:, rows, :], g.at[:, rows, :], g_sem.at[pair])

    for pair in range(PAIRS):
        g_copy(pair).start()
    e_copies, first_row = [], 0
    for i, block in enumerate(blocks):
        words = slice(first_row, first_row + block.shape[0])
        e_copies.append(pltpu.make_async_copy(block, e.at[words, :], e_sem.at[i]))
        first_row += block.shape[0]
    for copy in e_copies:
        copy.start()
    lane = lax.broadcasted_iota(jnp.int32, (16, 128), 1)

    def pair_step(pair, carry):
        g_copy(pair).wait()
        base = pair * PAIR_ROWS

        def tile(y, row):
            rows = pl.ds(pl.multiple_of(base + row, 16), 16)
            return g[y, rows, :].astype(jnp.float32)

        rest = [tile(y, 240) for y in range(NY)]
        for group in range(3):
            last = []
            for half in range(2):
                joined = None
                for q in range(4):
                    moved = rest[half * 4 + q]
                    shift = (q - group) * 32 % 128
                    if shift:
                        moved = pltpu.roll(moved, shift, 1)
                    joined = moved if joined is None else jnp.where(lane >= q * 32, moved, joined)
                last.append(joined)
            square = last[0] * last[0] + last[1] * last[1]
            for y in range(NY):
                for j in range(5):
                    value = tile(y, j * 48 + group * 16)
                    square = square + value * value
            scale = lax.rsqrt(jnp.sum(square, axis=1, keepdims=True) / H + epsilon)
            rows = pl.ds(pl.multiple_of(pair * 48 + group * 16, 16), 16)
            for y in range(NY):
                for j in range(5):
                    k = (y * 5 + j) * 128
                    value = tile(y, j * 48 + group * 16)
                    xn[rows, k : k + 128] = (value * scale * gain_ref[0:1, k : k + 128]).astype(jnp.bfloat16)
            for half in range(2):
                k = NY * FULL + half * 128
                xn[rows, k : k + 128] = (last[half] * scale * gain_ref[0:1, k : k + 128]).astype(jnp.bfloat16)
        return carry

    lax.fori_loop(0, PAIRS, pair_step, 0)

    for words, arrivals in ((slice(0, WORDS // 2), e_copies[:2]), (slice(WORDS // 2, WORDS), e_copies[2:])):
        for copy in arrivals:
            copy.wait()
        logits[:, words] = lax.dot_general(
            xn[...], e[words, :], (((1,), (1,)), ((), ())), preferred_element_type=jnp.float32
        )

    lane = lax.broadcasted_iota(jnp.int32, (48, 128), 1)
    stats = []
    for step in range(TOKENS // 48):
        rows = pl.ds(step * 48, 48)
        parts = [logits[rows, i * 128 : (i + 1) * 128] for i in range(WORDS // 128)]
        peak = parts[0]
        for part in parts[1:]:
            peak = jnp.maximum(peak, part)
        peak = jnp.max(peak, axis=1, keepdims=True)
        target = target_ref[rows, :]
        total = jnp.zeros((48, 128), jnp.float32)
        picked = jnp.zeros((48, 128), jnp.float32)
        for i, part in enumerate(parts):
            total = total + jnp.exp(part - peak)
            picked = picked + jnp.where(target - (place_ref[i // 2] + i % 2 * 128) == lane, part, 0.0)
        total = jnp.sum(total, axis=1, keepdims=True)
        picked = jnp.sum(picked, axis=1, keepdims=True)
        stats.append(jnp.where(lane == 0, peak, jnp.where(lane == 1, total, picked)))
    stats = jnp.concatenate(stats, axis=0)
    for i in range(TOKENS // 128):
        out_ref[:, i * 128 : (i + 1) * 128] = stats[i * 128 : (i + 1) * 128, :].T[0:8, :]


def local_losses(gathered, blocks, gain, target, place):
    any_space = pl.BlockSpec(memory_space=pl.ANY)
    vmem = pl.BlockSpec(memory_space=pltpu.VMEM)
    gathered = pltpu.with_memory_space_constraint(gathered, pltpu.HBM)
    blocks = [pltpu.with_memory_space_constraint(a, pltpu.HBM) for a in blocks]
    return pl.pallas_call(
        loss_kernel,
        out_shape=jax.ShapeDtypeStruct((8, TOKENS), jnp.float32),
        in_specs=[any_space] * 5 + [vmem, vmem, pl.BlockSpec(memory_space=pltpu.SMEM)],
        out_specs=vmem,
        scratch_shapes=[
            pltpu.VMEM((NY, PAIRS * PAIR_ROWS, 128), jnp.bfloat16),
            pltpu.VMEM((WORDS, H), jnp.bfloat16),
            pltpu.VMEM((TOKENS, H), jnp.bfloat16),
            pltpu.VMEM((TOKENS, WORDS), jnp.float32),
            pltpu.SemaphoreType.DMA((PAIRS,)),
            pltpu.SemaphoreType.DMA((len(blocks),)),
        ],
        compiler_params=pltpu.CompilerParams(vmem_limit_bytes=32 * 1024 * 1024),
        cost_estimate=pl.CostEstimate(flops=2 * TOKENS * WORDS * H, bytes_accessed=16 * 1024 * 1024, transcendentals=TOKENS * WORDS),
    )(gathered, *blocks, gain, target, place)


def prepare_kernel(hidden_ref, targets_ref, out_ref):
    row = lax.broadcasted_iota(jnp.int32, (24, 24), 0)
    column = lax.broadcasted_iota(jnp.int32, (24, 24), 1)
    lane = lax.broadcasted_iota(jnp.int32, (24, 128), 1)
    for m in range(2):
        target = jnp.sum(jnp.where(row == column, targets_ref[m : m + 1, :], 0), axis=1, keepdims=True)
        digits = jnp.where(lane == 80, target & 127, jnp.where(lane == 81, (target >> 7) & 127, target >> 14))
        tail = jnp.pad(hidden_ref[m, :, 256:336].astype(jnp.float32), ((0, 0), (0, 48)))
        tail = jnp.where(lane < 80, tail, jnp.where(lane < 83, digits.astype(jnp.float32), 0.0))
        tail = tail.astype(jnp.bfloat16)
        for s in range(SOURCES):
            out_ref[2 * s + m, :, 0:256] = hidden_ref[m, :, 0:256]
            out_ref[2 * s + m, :, 256:384] = tail


def prepare(hidden, targets):
    hidden, targets = (pltpu.with_memory_space_constraint(a, pltpu.HBM) for a in (hidden, targets))
    return pl.pallas_call(
        prepare_kernel,
        out_shape=pltpu.HBM((2 * SOURCES, 24, 384), jnp.bfloat16),
        compiler_params=SMALL,
    )(hidden, targets)


def repack_kernel(got_ref, units_ref, target_ref):
    lane = lax.broadcasted_iota(jnp.int32, (48, 128), 1)
    short = lane[0:16]
    weight = jnp.where(lane == 80, 1, jnp.where(lane == 81, 128, jnp.where(lane == 82, 16384, 0))).astype(jnp.float32)

    def pair_step(pair, carry):
        def tile(c, j):
            both = [got_ref[4 * pair + 2 * d + c, :, j * 128 : (j + 1) * 128].astype(jnp.float32) for d in range(2)]
            return jnp.concatenate(both, axis=0)

        a, b = tile(0, 2), tile(1, 2)
        tiles = [tile(0, 0), tile(0, 1), tile(1, 0), tile(1, 1), jnp.where(lane < 80, a, pltpu.roll(b, 80, 1))]
        base = pair * PAIR_ROWS
        for j in range(5):
            rows = pl.ds(pl.multiple_of(base + j * 48, 16), 48)
            units_ref[rows, :] = tiles[j].astype(jnp.bfloat16)
        rest = [pltpu.roll(b[g * 16 : (g + 1) * 16], (32 * g - 48) % 128, 1) for g in range(3)]
        rest = jnp.where(short < 32, rest[0], jnp.where(short < 64, rest[1], jnp.where(short < 96, rest[2], 0.0)))
        units_ref[pl.ds(pl.multiple_of(base + 240, 16), 16), :] = rest.astype(jnp.bfloat16)
        target = jnp.sum(a * weight, axis=1, keepdims=True)
        target_ref[pl.ds(pl.multiple_of(pair * 48, 16), 48), :] = target.astype(jnp.int32)
        return carry

    lax.fori_loop(0, PAIRS, pair_step, 0)


def repack(got):
    return pl.pallas_call(
        repack_kernel,
        out_shape=(
            pltpu.HBM((PAIRS * PAIR_ROWS, 128), jnp.bfloat16),
            jax.ShapeDtypeStruct((TOKENS, 1), jnp.int32),
        ),
        compiler_params=SMALL,
        cost_estimate=pl.CostEstimate(flops=2000000, bytes_accessed=1200000, transcendentals=0),
    )(got)


def pieces():
    for y in range(NY):
        for begin, end in ((0, 256), (336, 592), (256, 336), (592, 640)):
            yield y * PART + begin, y * PART + end
    for y in range(NY):
        yield y * PART + FULL, (y + 1) * PART


def arrange(tiles, lane):
    def window(begin):
        k, shift = divmod(begin, 128)
        if shift == 0:
            return tiles[k]
        after = pltpu.roll(tiles[(k + 1) % len(tiles)], 128 - shift, 1)
        return jnp.where(lane < 128 - shift, pltpu.roll(tiles[k], 128 - shift, 1), after)

    out = []
    for y in range(NY):
        at = y * PART
        out += [window(at), window(at + 128), window(at + 336), window(at + 464)]
        out.append(jnp.where(lane < 80, window(at + 256), window(at + 592 - 80)))
    for half in range(2):
        joined = None
        for q in range(4):
            k, shift = divmod((half * 4 + q) * PART + FULL, 128)
            moved = tiles[k]
            if (q * 32 - shift) % 128:
                moved = pltpu.roll(moved, (q * 32 - shift) % 128, 1)
            joined = moved if joined is None else jnp.where(lane >= q * 32, moved, joined)
        out.append(joined)
    return out


def arrange_gain_kernel(gain_ref, out_ref):
    lane = lax.broadcasted_iota(jnp.int32, (8, 128), 1)
    tiles = [jnp.broadcast_to(gain_ref[:, k * 128 : (k + 1) * 128], (8, 128)) for k in range(H // 128)]
    for k, tile in enumerate(arrange(tiles, lane)):
        out_ref[:, k * 128 : (k + 1) * 128] = tile


def arrange_gain(gain):
    return pl.pallas_call(
        arrange_gain_kernel, out_shape=jax.ShapeDtypeStruct((8, H), jnp.float32), compiler_params=SMALL
    )(gain.reshape(1, H))


def reorder_kernel(*refs):
    out_ref = refs[-1]
    before = 0
    for ref in refs[:-1]:
        block = ref.shape[0]
        lane = lax.broadcasted_iota(jnp.int32, (16, 128), 1)

        def step(i, carry):
            src = pl.ds(pl.multiple_of(i * 16, 16), 16)
            dst = pl.ds(pl.multiple_of(before + i * 16, 16), 16)
            tiles = [ref[src, k * 128 : (k + 1) * 128].astype(jnp.float32) for k in range(H // 128)]
            for k, tile in enumerate(arrange(tiles, lane)):
                out_ref[dst, k * 128 : (k + 1) * 128] = tile.astype(jnp.bfloat16)
            return carry

        lax.fori_loop(0, block // 16, step, 0)
        before += block


def reorder_rows(*rows):
    count = sum(r.shape[0] for r in rows)
    return pl.pallas_call(
        reorder_kernel,
        out_shape=jax.ShapeDtypeStruct((count, H), jnp.bfloat16),
        compiler_params=pltpu.CompilerParams(vmem_limit_bytes=16 * 1024 * 1024),
        cost_estimate=pl.CostEstimate(flops=count * H * 8, bytes_accessed=count * H * 4, transcendentals=0),
    )(*rows)


def combine(peak, total, picked, axis):
    top = jnp.max(peak, axis=axis)
    total = jnp.sum(total * jnp.exp(peak - jnp.expand_dims(top, axis)), axis=axis)
    return top, total, jnp.sum(picked, axis=axis)


def per_device(hidden, norm_gain, embedding, targets):
    swap = [(0, 1), (1, 0)]
    tie = lax.optimization_barrier
    xh, xl, z, y, core = (lax.axis_index(a) for a in ("xh", "xl", "z", "y", "core"))

    def first_row(low, c):
        return ((((xh * 2 + low) * 8 + z) * 8 + y) * 2 + c) * VOCAB_LOCAL

    near, beside, far, far_beside = (first_row(low, c) for low in (xl, 1 - xl) for c in (core, 1 - core))
    place = jnp.stack([near, beside, far, far_beside])

    payload, embedding = tie((prepare(hidden, targets), embedding))
    got = lax.all_to_all(payload, ("xh", "z", "core"), 0, 0, tiled=True)
    units, target = repack(got)

    rows1 = lax.ppermute(embedding[:EARLY], "xl", swap)
    units, late, rows1, gain = tie((units, embedding, rows1, norm_gain))
    gathered = lax.all_gather(units, "y", axis=0)

    rows2 = lax.ppermute(late[EARLY:], "xl", swap)
    own = reorder_rows(late)
    beside_rows = lax.ppermute(own, "core", swap)
    far_rows = reorder_rows(rows1, rows2)
    far_beside_rows = lax.ppermute(far_rows, "core", swap)
    blocks = (own, beside_rows, far_rows, far_beside_rows)
    stats = local_losses(gathered, blocks, arrange_gain(gain), target, place)
    stats = stats[:3].reshape(3, SOURCES, 24).transpose(1, 0, 2)
    stats = lax.all_to_all(stats, ("xh", "z"), 0, 0, tiled=True)
    part = jnp.stack(combine(stats[:, 0], stats[:, 1], stats[:, 2], 0))
    every = lax.all_to_all(jnp.broadcast_to(part[None], (16, 3, 24)), ("y", "core"), 0, 0, tiled=True)
    every = every.reshape(NY, 2, 3, 24)
    peak, total, picked = combine(every[:, :, 0], every[:, :, 1], every[:, :, 2], 0)
    return peak + jnp.log(total) - picked


def solution(mesh):
    fine = Mesh(mesh.devices.reshape(2, 2, 8, 8, 2), ("xh", "xl", "z", "y", "core"))
    dp, pipe = ("xh", "xl", "z"), ("y", "core")
    placed = (P(None, dp, pipe), P(), P(dp + pipe, None), P(None, dp))
    return jax.shard_map(per_device, mesh=fine, in_specs=placed, out_specs=P(None, dp), check_vma=False)
```

time: 407 us -> 160 us (0.39)
  blocking collectives: 261 us -> 33.8 us
  waiting for transfers between devices: 104 us -> 61 us
  starting transfers between devices: 0.01 us -> 26.9 us
  Pallas kernels: 0 us -> 21.1 us
  other arithmetic: 11.9 us -> 0.8 us
  local copies, waits for them, and re-layouts: 9.26 us -> 2.15 us
  matrix products: 6.02 us -> 0 us
    all_gather x1, waiting for transfers between devices: 104 us -> 0.01 us  [per_device(): gathered = lax.all_gather(units, 'y', axis=0)]
    pmax x1 -> x0, blocking collectives: 95.8 us -> none  [per_device(): global_peak = lax.pmax(row_peak, ('dp', 'pipe'))]
    psum x1 -> x0, blocking collectives: 94.4 us -> none  [per_device(): global_total, global_pick = lax.psum((shifted, picked), ('dp', 'pipe'))]
    all_gather x2 -> x0, blocking collectives: 71 us -> none  [the longest x1 37.4 us: per_device(): piece_targets = lax.all_gather(targets, 'dp', axis=1, tiled=True)]
    ppermute x0 -> x4, waiting for transfers between devices: none -> 45.8 us  [the longest x1 40.9 us: per_device(): rows2 = lax.ppermute(late[EARLY:], 'xl', swap)]
    all_to_all x0 -> x2, blocking collectives: none -> 33.8 us  [the longest x1 17.7 us: per_device(): stats = lax.all_to_all(stats, ('xh', 'z'), 0, 0, tiled=True)]
    pallas_call x0 -> x6, Pallas kernels: none -> 21.1 us  [the longest x1 10.5 us: local_losses(): pl.pallas_call(loss_kernel, out_shape=jax.ShapeDtypeStruct((8, TOKENS), j...]
    all_to_all x0 -> x1, waiting for transfers between devices: none -> 15.2 us  [per_device(): got = lax.all_to_all(payload, ('xh', 'z', 'core'), 0, 0, tiled=True)]
  transfers between devices with their start and end apart: 1 -> 6, of which waited for: 1 -> 4; matrix products, arithmetic and copies ran while one was open for 0% -> 1% of each run, Pallas kernels for 0% -> 5%
where the time goes in v1:
time: 160 us; the launch traced here: 159 us
  waiting for transfers between devices  61 us (38%)
  blocking collectives  33.8 us (21%)
  starting transfers between devices  26.9 us (17%)
  Pallas kernels  21.1 us (13%)
  between operations  13.6 us (8%)
  local copies, waits for them, and re-layouts  2.15 us (1%)
    ppermute x1, waiting for transfers between devices, per_device(): rows2 = lax.ppermute(late[EARLY:], 'xl', swap)  40.9 us
    all_to_all x1, blocking collectives, per_device(): stats = lax.all_to_all(stats, ('xh', 'z'), 0, 0, tiled=True)  17.7 us
    all_to_all x1, blocking collectives, per_device(): lax.all_to_all(jnp.broadcast_to(part[None], (16, 3, 24)), ('y', 'core'),...  16.1 us
    all_to_all x1, waiting for transfers between devices, per_device(): got = lax.all_to_all(payload, ('xh', 'z', 'core'), 0, 0, tiled=True)  15.2 us
    all_to_all x1, starting transfers between devices, per_device(): got = lax.all_to_all(payload, ('xh', 'z', 'core'), 0, 0, tiled=True)  14.4 us
    pallas_call x1, Pallas kernels, local_losses(): pl.pallas_call(loss_kernel, out_shape=jax.ShapeDtypeStruct((8, TOKENS), j...  10.5 us
    pallas_call x2, Pallas kernels, reorder_rows(): pl.pallas_call(reorder_kernel, out_shape=jax.ShapeDtypeStruct((count, H),...  6.96 us
    ppermute x1, waiting for transfers between devices, per_device(): far_beside_rows = lax.ppermute(far_rows, 'core', swap)  4.57 us
  transfers between devices with their start and end apart: 6, of which 4 were waited for; matrix products, arithmetic and copies ran while one was open for 1% of the time, Pallas kernels for 5%

profile of v1, /device:TPU:1, one launch (start us, length us, event | category | flops | bytes accessed | tf_op | source)
XLA Modules:
  0.0 159.2 jit_solution(5668067481034537880)
XLA Ops:
  6.5 0.0 copy-start
  6.5 1.8 %shard_map.46 = bf16[32,24,384]{2,1,0:T(8,128)(2,1)} custom-call(bf16[2,24,336]{2,1,0:T(8,128)(2,1)} %hidden_ref.1, s32[2,24]{1,0:T(2,128)} %targets_ref.1), custom_call_target="tpu_custom_call" | custom-call | tf_op jit(solution)/shard_map/pallas_call | solution.py:154
  8.4 14.4 %all-to-all-start = ((bf16[32,24,384]{2,1,0:T(8,128)(2,1)}), bf16[32,24,384]{2,1,0:T(8,128)(2,1)S(1)}, u32[]{:S(2)}, u32[]{:S(2)}) async-start(bf16[32,24,384]{2,1,0:T(8,128)(2,1)} %shard_map.46), calls=%async_computation | async-start | bytes 1179648 | tf_op jit(solution)/shard_map/all_to_all | solution.py:292
  22.8 0.0 all-gather.3.cloned.1.call-start
  22.9 1.9 %slice.27 = bf16[48,5376]{1,0:T(8,128)(2,1)} slice(bf16[256,5376]{1,0:T(8,128)(2,1)} %refs_0_), slice={[0:48], [0:5376]} | slice | bytes 1032192 | tf_op jit(solution)/shard_map/slice | solution.py:295
  24.7 2.2 %collective-permute-start = (bf16[48,5376]{1,0:T(8,128)(2,1)}, bf16[48,5376]{1,0:T(8,128)(2,1)}, u32[]{:S(2)}, u32[]{:S(2)}) collective-permute-start(bf16[48,5376]{1,0:T(8,128)(2,1)} %slice.27), channel_id=1, source_target_pairs={{0,128},{128,0},{1,129},{129,1},{2,130},{130,2},{3,131},{131,3},{4... | collective-permute-start | bytes 1548296 | tf_op jit(solution)/shard_map/ppermute | solution.py:295
  27.0 15.2 %all-to-all-done.got_ref = bf16[32,24,384]{2,1,0:T(8,128)(2,1)S(1)} async-done(((bf16[32,24,384]{2,1,0:T(8,128)(2,1)}), bf16[32,24,384]{2,1,0:T(8,128)(2,1)S(1)}, u32[]{:S(2)}, u32[]{:S(2)}) %all-to-all-start) | async-done | bytes 589856 | tf_op jit(solution)/shard_map/all_to_all | solution.py:292
  42.1 1.6 %shard_map.47 = (bf16[2048,128]{1,0:T(8,128)(2,1)}, s32[384,1]{1,0:T(8,128)S(1)}) custom-call(bf16[32,24,384]{2,1,0:T(8,128)(2,1)S(1)} %all-to-all-done.got_ref), custom_call_target="tpu_custom_call" | custom-call | flops 2000000 | bytes 1200000 | tf_op jit(solution)/shard_map/pallas_call | solution.py:188
  43.7 0.3 collective-permute-done.refs_0_
  44.1 0.0 all-gather.3.cloned.1.call-update
  44.1 0.0 copy-done
  44.1 0.1 slice.28
  44.3 3.4 %collective-permute-start.2 = (bf16[208,5376]{1,0:T(8,128)(2,1)S(1)}, bf16[208,5376]{1,0:T(8,128)(2,1)S(1)}, u32[]{:S(2)}, u32[]{:S(2)}) collective-permute-start(bf16[208,5376]{1,0:T(8,128)(2,1)S(1)} %slice.28), channel_id=1, source_target_pairs={{0,128},{128,0},{1,129},{129,1},{2,130},{130,2},{3,131},{131,3},{4... | collective-permute-start | bytes 6709256 | tf_op jit(solution)/shard_map/ppermute | solution.py:299
  47.7 3.8 %shard_map.48.refs_1_ = bf16[256,5376]{1,0:T(8,128)(2,1)} custom-call(bf16[256,5376]{1,0:T(8,128)(2,1)S(1)} %copy-done), custom_call_target="tpu_custom_call" | custom-call | flops 11010048 | bytes 5505024 | tf_op jit(solution)/shard_map/pallas_call | solution.py:266
  51.4 0.0 copy-start.2
  51.4 2.8 %collective-permute-start.1 = (bf16[256,5376]{1,0:T(8,128)(2,1)}, bf16[256,5376]{1,0:T(8,128)(2,1)}, u32[]{:S(2)}, u32[]{:S(2)}) collective-permute-start(bf16[256,5376]{1,0:T(8,128)(2,1)} %shard_map.48.refs_1_), channel_id=1, source_target_pairs={{0,1},{1,0},{2,3},{3,2},{4,5},{5,4},{6,7},{7,6},{8,9},{9,8},{10,11... | collective-permute-start | bytes 8257544 | tf_op jit(solution)/shard_map/ppermute | solution.py:301
  54.3 40.9 %collective-permute-done.2.refs_1_ = bf16[208,5376]{1,0:T(8,128)(2,1)S(1)} collective-permute-done((bf16[208,5376]{1,0:T(8,128)(2,1)S(1)}, bf16[208,5376]{1,0:T(8,128)(2,1)S(1)}, u32[]{:S(2)}, u32[]{:S(2)}) %collective-permute-start.2) | collective-permute-done | bytes 2236448 | tf_op jit(solution)/shard_map/ppermute | solution.py:299
  95.1 3.2 %shard_map.49.refs_3_ = bf16[256,5376]{1,0:T(8,128)(2,1)S(1)} custom-call(bf16[48,5376]{1,0:T(8,128)(2,1)} %collective-permute-done.refs_0_, bf16[208,5376]{1,0:T(8,128)(2,1)S(1)} %collective-permute-done.2.refs_1_), custom_call_target="tpu_custom_call" | custom-call | flops 11010048 | bytes 5505024 | tf_op jit(solution)/shard_map/pallas_call | solution.py:266
  98.3 0.0 copy-start.1
  98.3 4.0 %collective-permute-start.3 = (bf16[256,5376]{1,0:T(8,128)(2,1)S(1)}, bf16[256,5376]{1,0:T(8,128)(2,1)}, u32[]{:S(2)}, u32[]{:S(2)}) collective-permute-start(bf16[256,5376]{1,0:T(8,128)(2,1)S(1)} %shard_map.49.refs_3_), channel_id=1, source_target_pairs={{0,1},{1,0},{2,3},{3,2},{4,5},{5,4},{6,7},{7,6},{8,9},{9,8},{10,11... | collective-permute-start | bytes 8257544 | tf_op jit(solution)/shard_map/ppermute | solution.py:303
  102.4 0.1 pad_add_fusion.refs_7_
  102.4 0.0 copy-done.2
  102.5 0.1 shard_map.50.refs_5_
  102.6 0.0 collective-permute-done.1.refs_2_
  102.6 4.6 %collective-permute-done.3.refs_4_ = bf16[256,5376]{1,0:T(8,128)(2,1)} collective-permute-done((bf16[256,5376]{1,0:T(8,128)(2,1)S(1)}, bf16[256,5376]{1,0:T(8,128)(2,1)}, u32[]{:S(2)}, u32[]{:S(2)}) %collective-permute-start.3) | collective-permute-done | bytes 2752544 | tf_op jit(solution)/shard_map/ppermute | solution.py:303
  107.2 0.0 all-gather.3.cloned.1.call-done
  107.2 0.0 copy-done.1
  107.2 10.5 %shard_map.51 = f32[8,384]{1,0:T(8,128)S(1)} custom-call(bf16[8,2048,128]{2,1,0:T(8,128)(2,1)} %bitcast.37, bf16[256,5376]{1,0:T(8,128)(2,1)} %shard_map.48.refs_1_, bf16[256,5376]{1,0:T(8,128)(2,1)} %collective-permute-done.1.refs_2_, bf16[256,5376]{1,0:T(8,128)(2,1)} %copy-done.1, bf16[256,5376]{1,0:T(8,128)(2,1)} %collective-permute-done.3.refs_4_, ...), custom_call_target="tpu_custom_call" | custom-call | flops 4227858432 | bytes 16777216 | tf_op jit(solution)/shard_map/pallas_call | solution.py:119
  117.7 0.1 reshape.13
  117.9 17.7 %all_to_all.15 = f32[16,3,24]{2,1,0:T(4,128)S(1)} all-to-all(f32[16,3,24]{2,1,0:T(4,128)S(1)} %bitcast.30), channel_id=1, replica_groups=mesh['xh'=2,'xl'=2,'z'=8,'y'=8,'core'=2] {'xh','z'}, dimensions={0} | all-to-all | bytes 9216 | tf_op jit(solution)/shard_map/all_to_all | solution.py:307
  135.7 16.1 %all_to_all.16 = f32[16,3,24]{2,1,0:T(4,128)S(1)} all-to-all(f32[16,3,24]{2,1,0:T(4,128)S(1)} %broadcast_in_dim.2), channel_id=1, replica_groups=mesh['xh'=2,'xl'=2,'z'=8,'y'=8,'core'=2] {'y','core'}, dimensions={0} | all-to-all | bytes 9216 | tf_op jit(solution)/shard_map/all_to_all | solution.py:309
  151.8 0.6 add_subtract_fusion
  (11 shorter events, 0.2 us)
Async XLA Ops:
  6.5 37.6 %copy-start = (bf16[256,5376]{1,0:T(8,128)(2,1)S(1)}, bf16[256,5376]{1,0:T(8,128)(2,1)}, u32[]{:S(2)}) copy-start(bf16[256,5376]{1,0:T(8,128)(2,1)} %refs_0_) | copy-start | bytes 8257540
  8.4 33.7 %all-to-all-start = ((bf16[32,24,384]{2,1,0:T(8,128)(2,1)}), bf16[32,24,384]{2,1,0:T(8,128)(2,1)S(1)}, u32[]{:S(2)}, u32[]{:S(2)}) async-start(bf16[32,24,384]{2,1,0:T(8,128)(2,1)} %shard_map.46), calls=%async_computation | async-start | bytes 1179648 | tf_op jit(solution)/shard_map/all_to_all | solution.py:292
  22.8 84.4 %all-gather.3.cloned.1.call-start = ((), (), s32[]{:S(2)}) async-start(), calls=%async_computation.3 | async-start | bytes 4718592 | tf_op jit(solution)/shard_map/all_gather | solution.py:297
  24.7 19.3 %collective-permute-start = (bf16[48,5376]{1,0:T(8,128)(2,1)}, bf16[48,5376]{1,0:T(8,128)(2,1)}, u32[]{:S(2)}, u32[]{:S(2)}) collective-permute-start(bf16[48,5376]{1,0:T(8,128)(2,1)} %slice.27), channel_id=1, source_target_pairs={{0,128},{128,0},{1,129},{129,1},{2,130},{130,2},{3,131},{131,3},{4... | collective-permute-start | bytes 1548296 | tf_op jit(solution)/shard_map/ppermute | solution.py:295
  44.3 50.9 %collective-permute-start.2 = (bf16[208,5376]{1,0:T(8,128)(2,1)S(1)}, bf16[208,5376]{1,0:T(8,128)(2,1)S(1)}, u32[]{:S(2)}, u32[]{:S(2)}) collective-permute-start(bf16[208,5376]{1,0:T(8,128)(2,1)S(1)} %slice.28), channel_id=1, source_target_pairs={{0,128},{128,0},{1,129},{129,1},{2,130},{130,2},{3,131},{131,3},{4... | collective-permute-start | bytes 6709256 | tf_op jit(solution)/shard_map/ppermute | solution.py:299
  51.4 51.0 %copy-start.2 = (f32[5376]{0:T(1024)S(1)}, f32[5376]{0:T(1024)}, u32[]{:S(2)}) copy-start(f32[5376]{0:T(1024)} %param.5) | copy-start | bytes 64516
  51.4 51.2 %collective-permute-start.1 = (bf16[256,5376]{1,0:T(8,128)(2,1)}, bf16[256,5376]{1,0:T(8,128)(2,1)}, u32[]{:S(2)}, u32[]{:S(2)}) collective-permute-start(bf16[256,5376]{1,0:T(8,128)(2,1)} %shard_map.48.refs_1_), channel_id=1, source_target_pairs={{0,1},{1,0},{2,3},{3,2},{4,5},{5,4},{6,7},{7,6},{8,9},{9,8},{10,11... | collective-permute-start | bytes 8257544 | tf_op jit(solution)/shard_map/ppermute | solution.py:301
  98.3 8.9 %copy-start.1 = (bf16[256,5376]{1,0:T(8,128)(2,1)}, bf16[256,5376]{1,0:T(8,128)(2,1)S(1)}, u32[]{:S(2)}) copy-start(bf16[256,5376]{1,0:T(8,128)(2,1)S(1)} %shard_map.49.refs_3_) | copy-start | bytes 8257540
  98.3 8.9 %collective-permute-start.3 = (bf16[256,5376]{1,0:T(8,128)(2,1)S(1)}, bf16[256,5376]{1,0:T(8,128)(2,1)}, u32[]{:S(2)}, u32[]{:S(2)}) collective-permute-start(bf16[256,5376]{1,0:T(8,128)(2,1)S(1)} %shard_map.49.refs_3_), channel_id=1, source_target_pairs={{0,1},{1,0},{2,3},{3,2},{4,5},{5,4},{6,7},{7,6},{8,9},{9,8},{10,11... | collective-permute-start | bytes 8257544 | tf_op jit(solution)/shard_map/ppermute | solution.py:303
Sparse Core Ops, SparseCore 0:
  44.2 58.2 all-gather.2

commit v2 on v1

--- a/solution.py
+++ b/solution.py
@@ -18,14 +18,14 @@
 PAIRS = SOURCES // 2
 PAIR_ROWS = 256
 VOCAB_LOCAL = 256
-EARLY = 48
+PIECE = VOCAB_LOCAL // 2
 WORDS = 4 * VOCAB_LOCAL
 SMALL = pltpu.CompilerParams(vmem_limit_bytes=8 * 1024 * 1024)
 
 
 def loss_kernel(*refs):
-    g_any, blocks = refs[0], refs[1:5]
-    gain_ref, target_ref, place_ref, out_ref, g, e, xn, logits, g_sem, e_sem = refs[5:]
+    g_any, blocks = refs[0], refs[1:9]
+    gain_ref, target_ref, place_ref, out_ref, g, e, xn, logits, g_sem, e_sem = refs[9:]
 
     def g_copy(pair):
         rows = pl.ds(pl.multiple_of(pair * PAIR_ROWS, PAIR_ROWS), PAIR_ROWS)
@@ -81,7 +81,7 @@
 
     lax.fori_loop(0, PAIRS, pair_step, 0)
 
-    for words, arrivals in ((slice(0, WORDS // 2), e_copies[:2]), (slice(WORDS // 2, WORDS), e_copies[2:])):
+    for words, arrivals in ((slice(0, WORDS // 2), e_copies[:4]), (slice(WORDS // 2, WORDS), e_copies[4:])):
         for copy in arrivals:
             copy.wait()
         logits[:, words] = lax.dot_general(
@@ -102,7 +102,7 @@
         picked = jnp.zeros((48, 128), jnp.float32)
         for i, part in enumerate(parts):
             total = total + jnp.exp(part - peak)
-            picked = picked + jnp.where(target - (place_ref[i // 2] + i % 2 * 128) == lane, part, 0.0)
+            picked = picked + jnp.where(target - place_ref[i] == lane, part, 0.0)
         total = jnp.sum(total, axis=1, keepdims=True)
         picked = jnp.sum(picked, axis=1, keepdims=True)
         stats.append(jnp.where(lane == 0, peak, jnp.where(lane == 1, total, picked)))
@@ -119,7 +119,7 @@
     return pl.pallas_call(
         loss_kernel,
         out_shape=jax.ShapeDtypeStruct((8, TOKENS), jnp.float32),
-        in_specs=[any_space] * 5 + [vmem, vmem, pl.BlockSpec(memory_space=pltpu.SMEM)],
+        in_specs=[any_space] * 9 + [vmem, vmem, pl.BlockSpec(memory_space=pltpu.SMEM)],
         out_specs=vmem,
         scratch_shapes=[
             pltpu.VMEM((NY, PAIRS * PAIR_ROWS, 128), jnp.bfloat16),
@@ -242,33 +242,29 @@
     )(gain.reshape(1, H))
 
 
-def reorder_kernel(*refs):
-    out_ref = refs[-1]
-    before = 0
-    for ref in refs[:-1]:
-        block = ref.shape[0]
-        lane = lax.broadcasted_iota(jnp.int32, (16, 128), 1)
+def reorder_kernel(ref, *out_refs):
+    lane = lax.broadcasted_iota(jnp.int32, (16, 128), 1)
+    for n, out_ref in enumerate(out_refs):
 
         def step(i, carry):
-            src = pl.ds(pl.multiple_of(i * 16, 16), 16)
-            dst = pl.ds(pl.multiple_of(before + i * 16, 16), 16)
+            src = pl.ds(pl.multiple_of(n * PIECE + i * 16, 16), 16)
+            dst = pl.ds(pl.multiple_of(i * 16, 16), 16)
             tiles = [ref[src, k * 128 : (k + 1) * 128].astype(jnp.float32) for k in range(H // 128)]
             for k, tile in enumerate(arrange(tiles, lane)):
                 out_ref[dst, k * 128 : (k + 1) * 128] = tile.astype(jnp.bfloat16)
             return carry
 
-        lax.fori_loop(0, block // 16, step, 0)
-        before += block
-
-
-def reorder_rows(*rows):
-    count = sum(r.shape[0] for r in rows)
+        lax.fori_loop(0, PIECE // 16, step, 0)
+
+
+def reorder_rows(rows):
+    piece = jax.ShapeDtypeStruct((PIECE, H), jnp.bfloat16)
     return pl.pallas_call(
         reorder_kernel,
-        out_shape=jax.ShapeDtypeStruct((count, H), jnp.bfloat16),
+        out_shape=(piece, piece),
         compiler_params=pltpu.CompilerParams(vmem_limit_bytes=16 * 1024 * 1024),
-        cost_estimate=pl.CostEstimate(flops=count * H * 8, bytes_accessed=count * H * 4, transcendentals=0),
-    )(*rows)
+        cost_estimate=pl.CostEstimate(flops=VOCAB_LOCAL * H * 8, bytes_accessed=VOCAB_LOCAL * H * 4, transcendentals=0),
+    )(rows)
 
 
 def combine(peak, total, picked, axis):
@@ -282,27 +278,29 @@
     tie = lax.optimization_barrier
     xh, xl, z, y, core = (lax.axis_index(a) for a in ("xh", "xl", "z", "y", "core"))
 
-    def first_row(low, c):
-        return ((((xh * 2 + low) * 8 + z) * 8 + y) * 2 + c) * VOCAB_LOCAL
-
-    near, beside, far, far_beside = (first_row(low, c) for low in (xl, 1 - xl) for c in (core, 1 - core))
-    place = jnp.stack([near, beside, far, far_beside])
+    x = xh * 2 + xl
+
+    def first_row(at, c):
+        return (((at % 4 * 8 + z) * 8 + y) * 2 + c) * VOCAB_LOCAL
+
+    near = [first_row(x, c) + n * PIECE for c in (core, 1 - core) for n in range(2)]
+    far = [first_row(x + 3 - 2 * n, c) + n * PIECE for c in (core, 1 - core) for n in range(2)]
+    place = jnp.stack(near + far)
 
     payload, embedding = tie((prepare(hidden, targets), embedding))
     got = lax.all_to_all(payload, ("xh", "z", "core"), 0, 0, tiled=True)
     units, target = repack(got)
 
-    rows1 = lax.ppermute(embedding[:EARLY], "xl", swap)
-    units, late, rows1, gain = tie((units, embedding, rows1, norm_gain))
+    units, late, gain = tie((units, embedding, norm_gain))
     gathered = lax.all_gather(units, "y", axis=0)
 
-    rows2 = lax.ppermute(late[EARLY:], "xl", swap)
-    own = reorder_rows(late)
-    beside_rows = lax.ppermute(own, "core", swap)
-    far_rows = reorder_rows(rows1, rows2)
-    far_beside_rows = lax.ppermute(far_rows, "core", swap)
-    blocks = (own, beside_rows, far_rows, far_beside_rows)
-    stats = local_losses(gathered, blocks, arrange_gain(gain), target, place)
+    low, high = reorder_rows(late)
+    from_left = lax.ppermute(low, ("xh", "xl"), [(i, (i + 1) % 4) for i in range(4)])
+    from_right = lax.ppermute(high, ("xh", "xl"), [(i, (i - 1) % 4) for i in range(4)])
+    near, far = [low, high], [from_left, from_right]
+    near += [lax.ppermute(rows, "core", swap) for rows in near]
+    far += [lax.ppermute(rows, "core", swap) for rows in far]
+    stats = local_losses(gathered, near + far, arrange_gain(gain), target, place)
     stats = stats[:3].reshape(3, SOURCES, 24).transpose(1, 0, 2)
     stats = lax.all_to_all(stats, ("xh", "z"), 0, 0, tiled=True)
     part = jnp.stack(combine(stats[:, 0], stats[:, 1], stats[:, 2], 0))

time: 160 us -> 148 us (0.925)
  blocking collectives: 33.8 us -> 65.8 us
  waiting for transfers between devices: 61 us -> 29.7 us
  starting transfers between devices: 26.9 us -> 19.5 us
  Pallas kernels: 21.1 us -> 18.2 us
  local copies, waits for them, and re-layouts: 2.15 us -> 0.23 us
    all_to_all x0 -> x1, blocking collectives: none -> 33.7 us  [per_device(): got = lax.all_to_all(payload, ('xh', 'z', 'core'), 0, 0, tiled=True)]
    ppermute x4 -> x6, waiting for transfers between devices: 45.8 us -> 23.3 us  [the longest x1 20.2 us: per_device(): lax.ppermute(low, ('xh', 'xl'), [(i, (i + 1) % 4) for i in range(4)])]
    all_to_all x1 -> x0, waiting for transfers between devices: 15.2 us -> none  [per_device(): got = lax.all_to_all(payload, ('xh', 'z', 'core'), 0, 0, tiled=True)]
    all_to_all x1 -> x0, starting transfers between devices: 14.4 us -> none  [per_device(): got = lax.all_to_all(payload, ('xh', 'z', 'core'), 0, 0, tiled=True)]
    ppermute x4 -> x6, starting transfers between devices: 12.4 us -> 19.5 us  [the longest x2 6.63 us: per_device(): far += [lax.ppermute(rows, 'core', swap) for rows in far]]
    all_gather x1, waiting for transfers between devices: 0.01 us -> 6.38 us  [per_device(): gathered = lax.all_gather(units, 'y', axis=0)]
    pallas_call x2 -> x1, Pallas kernels: 6.96 us -> 3.63 us  [reorder_rows(): pl.pallas_call(reorder_kernel, out_shape=(piece, piece), compiler_params=...]
    all_to_all x1, blocking collectives: 16.1 us -> 13.8 us  [per_device(): lax.all_to_all(jnp.broadcast_to(part[None], (16, 3, 24)), ('y', 'core'),...]
  transfers between devices with their start and end apart: 6 -> 7, of which waited for: 4 -> 4; matrix products, arithmetic and copies ran while one was open for 1% -> 0% of each run, Pallas kernels for 5% -> 3%
where the time goes in v2:
time: 148 us
  blocking collectives  65.8 us (44%)
  waiting for transfers between devices  29.7 us (20%)
  starting transfers between devices  19.5 us (13%)
  Pallas kernels  18.2 us (12%)
  between operations  13.6 us (9%)
    all_to_all x1, blocking collectives, per_device(): got = lax.all_to_all(payload, ('xh', 'z', 'core'), 0, 0, tiled=True)  33.7 us
    ppermute x1, waiting for transfers between devices, per_device(): lax.ppermute(low, ('xh', 'xl'), [(i, (i + 1) % 4) for i in range(4)])  20.2 us
    all_to_all x1, blocking collectives, per_device(): stats = lax.all_to_all(stats, ('xh', 'z'), 0, 0, tiled=True)  18.3 us
    all_to_all x1, blocking collectives, per_device(): lax.all_to_all(jnp.broadcast_to(part[None], (16, 3, 24)), ('y', 'core'),...  13.8 us
    pallas_call x1, Pallas kernels, local_losses(): pl.pallas_call(loss_kernel, out_shape=jax.ShapeDtypeStruct((8, TOKENS), j...  11 us
    ppermute x2, starting transfers between devices, per_device(): far += [lax.ppermute(rows, 'core', swap) for rows in far]  6.63 us
    ppermute x2, starting transfers between devices, per_device(): near += [lax.ppermute(rows, 'core', swap) for rows in near]  6.38 us
    all_gather x1, waiting for transfers between devices, per_device(): gathered = lax.all_gather(units, 'y', axis=0)  6.38 us
  transfers between devices with their start and end apart: 7, of which 4 were waited for; matrix products, arithmetic and copies ran while one was open for 0% of the time, Pallas kernels for 3%

profile of v2, /device:TPU:1, one launch (start us, length us, event | category | flops | bytes accessed | tf_op | source)
XLA Modules:
  0.0 147.7 jit_solution(14925209849879748304)
XLA Ops:
  6.5 0.0 copy-start
  6.5 0.0 all-gather.3.cloned.1.call-start
  6.5 1.8 %shard_map.46 = bf16[32,24,384]{2,1,0:T(8,128)(2,1)} custom-call(bf16[2,24,336]{2,1,0:T(8,128)(2,1)} %hidden_ref.1, s32[2,24]{1,0:T(2,128)} %targets_ref.1), custom_call_target="tpu_custom_call" | custom-call | tf_op jit(solution)/shard_map/pallas_call | solution.py:154
  8.4 33.7 %all_to_all.15.got_ref = bf16[32,24,384]{2,1,0:T(8,128)(2,1)S(1)} all-to-all(bf16[32,24,384]{2,1,0:T(8,128)(2,1)} %shard_map.46), channel_id=1, replica_groups=mesh['xh'=2,'xl'=2,'z'=8,'y'=8,'core'=2] {'xh','z','core'}, dimensions={0} | all-to-all | bytes 1179648 | tf_op jit(solution)/shard_map/all_to_all | solution.py:291
  42.1 1.6 %shard_map.47 = (bf16[2048,128]{1,0:T(8,128)(2,1)}, s32[384,1]{1,0:T(8,128)S(1)}) custom-call(bf16[32,24,384]{2,1,0:T(8,128)(2,1)S(1)} %all_to_all.15.got_ref), custom_call_target="tpu_custom_call" | custom-call | flops 2000000 | bytes 1200000 | tf_op jit(solution)/shard_map/pallas_call | solution.py:188
  43.7 0.0 all-gather.3.cloned.1.call-update
  43.7 0.0 copy-done
  43.7 0.0 copy-start.1
  43.8 3.6 %shard_map.48 = (bf16[128,5376]{1,0:T(8,128)(2,1)}, bf16[128,5376]{1,0:T(8,128)(2,1)}) custom-call(bf16[256,5376]{1,0:T(8,128)(2,1)S(1)} %copy-done), custom_call_target="tpu_custom_call" | custom-call | flops 11010048 | bytes 5505024 | tf_op jit(solution)/shard_map/pallas_call | solution.py:262
  47.4 2.2 %collective-permute-start.2 = (bf16[128,5376]{1,0:T(8,128)(2,1)}, bf16[128,5376]{1,0:T(8,128)(2,1)S(1)}, u32[]{:S(2)}, u32[]{:S(2)}) collective-permute-start(bf16[128,5376]{1,0:T(8,128)(2,1)} %get-tuple-element.19.refs_1_), channel_id=1, source_target_pairs={{0,128},{128,256},{256,384},{384,0},{1,129},{129,257},{257,385},{3... | collective-permute-start | bytes 4128776 | tf_op jit(solution)/shard_map/ppermute | solution.py:298
  49.6 4.3 %collective-permute-start.3 = (bf16[128,5376]{1,0:T(8,128)(2,1)}, bf16[128,5376]{1,0:T(8,128)(2,1)}, u32[]{:S(2)}, u32[]{:S(2)}) collective-permute-start(bf16[128,5376]{1,0:T(8,128)(2,1)} %get-tuple-element.20.refs_2_), channel_id=1, source_target_pairs={{0,384},{128,0},{256,128},{384,256},{1,385},{129,1},{257,129},{385... | collective-permute-start | bytes 4128776 | tf_op jit(solution)/shard_map/ppermute | solution.py:299
  53.9 4.5 %collective-permute-start = (bf16[128,5376]{1,0:T(8,128)(2,1)}, bf16[128,5376]{1,0:T(8,128)(2,1)}, u32[]{:S(2)}, u32[]{:S(2)}) collective-permute-start(bf16[128,5376]{1,0:T(8,128)(2,1)} %get-tuple-element.19.refs_1_), channel_id=1, source_target_pairs={{0,1},{1,0},{2,3},{3,2},{4,5},{5,4},{6,7},{7,6},{8,9},{9,8},{10,11... | collective-permute-start | bytes 4128776 | tf_op jit(solution)/shard_map/ppermute | solution.py:301
  58.3 1.9 %collective-permute-start.1 = (bf16[128,5376]{1,0:T(8,128)(2,1)}, bf16[128,5376]{1,0:T(8,128)(2,1)}, u32[]{:S(2)}, u32[]{:S(2)}) collective-permute-start(bf16[128,5376]{1,0:T(8,128)(2,1)} %get-tuple-element.20.refs_2_), channel_id=1, source_target_pairs={{0,1},{1,0},{2,3},{3,2},{4,5},{5,4},{6,7},{7,6},{8,9},{9,8},{10,11... | collective-permute-start | bytes 4128776 | tf_op jit(solution)/shard_map/ppermute | solution.py:301
  60.3 20.2 %collective-permute-done.2.refs_5_ = bf16[128,5376]{1,0:T(8,128)(2,1)S(1)} collective-permute-done((bf16[128,5376]{1,0:T(8,128)(2,1)}, bf16[128,5376]{1,0:T(8,128)(2,1)S(1)}, u32[]{:S(2)}, u32[]{:S(2)}) %collective-permute-start.2) | collective-permute-done | bytes 1376288 | tf_op jit(solution)/shard_map/ppermute | solution.py:298
  80.5 0.0 copy-start.2
  80.5 4.7 %collective-permute-start.4 = (bf16[128,5376]{1,0:T(8,128)(2,1)S(1)}, bf16[128,5376]{1,0:T(8,128)(2,1)}, u32[]{:S(2)}, u32[]{:S(2)}) collective-permute-start(bf16[128,5376]{1,0:T(8,128)(2,1)S(1)} %collective-permute-done.2.refs_5_), channel_id=1, source_target_pairs={{0,1},{1,0},{2,3},{3,2},{4,5},{5,4},{6,7},{7,6},{8,9},{9,8},{10,11... | collective-permute-start | bytes 4128776 | tf_op jit(solution)/shard_map/ppermute | solution.py:302
  85.2 0.0 collective-permute-done.3.refs_6_
  85.2 1.9 %collective-permute-start.5 = (bf16[128,5376]{1,0:T(8,128)(2,1)}, bf16[128,5376]{1,0:T(8,128)(2,1)}, u32[]{:S(2)}, u32[]{:S(2)}) collective-permute-start(bf16[128,5376]{1,0:T(8,128)(2,1)} %collective-permute-done.3.refs_6_), channel_id=1, source_target_pairs={{0,1},{1,0},{2,3},{3,2},{4,5},{5,4},{6,7},{7,6},{8,9},{9,8},{10,11... | collective-permute-start | bytes 4128776 | tf_op jit(solution)/shard_map/ppermute | solution.py:302
  87.2 0.1 stack.47.refs_11_
  87.3 0.0 copy-done.1
  87.3 0.1 shard_map.49.refs_9_
  87.4 0.0 collective-permute-done.refs_3_
  87.4 0.0 collective-permute-done.1.refs_4_
  87.4 0.6 collective-permute-done.4.refs_7_
  88.1 2.5 %collective-permute-done.5.refs_8_ = bf16[128,5376]{1,0:T(8,128)(2,1)} collective-permute-done((bf16[128,5376]{1,0:T(8,128)(2,1)}, bf16[128,5376]{1,0:T(8,128)(2,1)}, u32[]{:S(2)}, u32[]{:S(2)}) %collective-permute-start.5) | collective-permute-done | bytes 1376288 | tf_op jit(solution)/shard_map/ppermute | solution.py:302
  90.6 6.4 %all-gather.3.cloned.1.call-done = bf16[16384,128]{1,0:T(8,128)(2,1)} async-done(((bf16[2048,128]{1,0:T(8,128)(2,1)}), bf16[16384,128]{1,0:T(8,128)(2,1)}) %all-gather.3.cloned.1.call-update) | async-done | bytes 4194320 | tf_op jit(solution)/shard_map/all_gather | solution.py:295
  96.9 0.0 copy-done.2
  96.9 11.0 %shard_map.50 = f32[8,384]{1,0:T(8,128)S(1)} custom-call(bf16[8,2048,128]{2,1,0:T(8,128)(2,1)} %bitcast.41, bf16[128,5376]{1,0:T(8,128)(2,1)} %get-tuple-element.19.refs_1_, bf16[128,5376]{1,0:T(8,128)(2,1)} %get-tuple-element.20.refs_2_, bf16[128,5376]{1,0:T(8,128)(2,1)} %collective-permute-done.refs_3_, bf16[128,5376]{1,0:T(8,128)(2,1)} %collective-permute-done.1.refs_4_, ...), custom_call_target="tpu_custom_call" | custom-call | flops 4227858432 | bytes 16777216 | tf_op jit(solution)/shard_map/pallas_call | solution.py:119
  107.9 0.1 reshape.13
  108.0 18.3 %all_to_all.16 = f32[16,3,24]{2,1,0:T(4,128)S(1)} all-to-all(f32[16,3,24]{2,1,0:T(4,128)S(1)} %bitcast.34), channel_id=1, replica_groups=mesh['xh'=2,'xl'=2,'z'=8,'y'=8,'core'=2] {'xh','z'}, dimensions={0} | all-to-all | bytes 9216 | tf_op jit(solution)/shard_map/all_to_all | solution.py:305
  126.4 13.8 %all_to_all.17 = f32[16,3,24]{2,1,0:T(4,128)S(1)} all-to-all(f32[16,3,24]{2,1,0:T(4,128)S(1)} %broadcast_in_dim.2), channel_id=1, replica_groups=mesh['xh'=2,'xl'=2,'z'=8,'y'=8,'core'=2] {'y','core'}, dimensions={0} | all-to-all | bytes 9216 | tf_op jit(solution)/shard_map/all_to_all | solution.py:307
  140.2 0.6 add_subtract_fusion
  (11 shorter events, 0.2 us)
Async XLA Ops:
  6.5 37.2 %copy-start = (bf16[256,5376]{1,0:T(8,128)(2,1)S(1)}, bf16[256,5376]{1,0:T(8,128)(2,1)}, u32[]{:S(2)}) copy-start(bf16[256,5376]{1,0:T(8,128)(2,1)} %ref) | copy-start | bytes 8257540
  6.5 90.4 %all-gather.3.cloned.1.call-start = ((), (), s32[]{:S(2)}) async-start(), calls=%async_computation.3 | async-start | bytes 4718592 | tf_op jit(solution)/shard_map/all_gather | solution.py:295
  43.7 43.5 %copy-start.1 = (f32[5376]{0:T(1024)S(1)}, f32[5376]{0:T(1024)}, u32[]{:S(2)}) copy-start(f32[5376]{0:T(1024)} %param.5) | copy-start | bytes 64516
  47.4 33.1 %collective-permute-start.2 = (bf16[128,5376]{1,0:T(8,128)(2,1)}, bf16[128,5376]{1,0:T(8,128)(2,1)S(1)}, u32[]{:S(2)}, u32[]{:S(2)}) collective-permute-start(bf16[128,5376]{1,0:T(8,128)(2,1)} %get-tuple-element.19.refs_1_), channel_id=1, source_target_pairs={{0,128},{128,256},{256,384},{384,0},{1,129},{129,257},{257,385},{3... | collective-permute-start | bytes 4128776 | tf_op jit(solution)/shard_map/ppermute | solution.py:298
  49.6 35.6 %collective-permute-start.3 = (bf16[128,5376]{1,0:T(8,128)(2,1)}, bf16[128,5376]{1,0:T(8,128)(2,1)}, u32[]{:S(2)}, u32[]{:S(2)}) collective-permute-start(bf16[128,5376]{1,0:T(8,128)(2,1)} %get-tuple-element.20.refs_2_), channel_id=1, source_target_pairs={{0,384},{128,0},{256,128},{384,256},{1,385},{129,1},{257,129},{385... | collective-permute-start | bytes 4128776 | tf_op jit(solution)/shard_map/ppermute | solution.py:299
  53.9 33.5 %collective-permute-start = (bf16[128,5376]{1,0:T(8,128)(2,1)}, bf16[128,5376]{1,0:T(8,128)(2,1)}, u32[]{:S(2)}, u32[]{:S(2)}) collective-permute-start(bf16[128,5376]{1,0:T(8,128)(2,1)} %get-tuple-element.19.refs_1_), channel_id=1, source_target_pairs={{0,1},{1,0},{2,3},{3,2},{4,5},{5,4},{6,7},{7,6},{8,9},{9,8},{10,11... | collective-permute-start | bytes 4128776 | tf_op jit(solution)/shard_map/ppermute | solution.py:301
  58.3 29.1 %collective-permute-start.1 = (bf16[128,5376]{1,0:T(8,128)(2,1)}, bf16[128,5376]{1,0:T(8,128)(2,1)}, u32[]{:S(2)}, u32[]{:S(2)}) collective-permute-start(bf16[128,5376]{1,0:T(8,128)(2,1)} %get-tuple-element.20.refs_2_), channel_id=1, source_target_pairs={{0,1},{1,0},{2,3},{3,2},{4,5},{5,4},{6,7},{7,6},{8,9},{9,8},{10,11... | collective-permute-start | bytes 4128776 | tf_op jit(solution)/shard_map/ppermute | solution.py:301
  80.5 16.5 %copy-start.2 = (bf16[128,5376]{1,0:T(8,128)(2,1)}, bf16[128,5376]{1,0:T(8,128)(2,1)S(1)}, u32[]{:S(2)}) copy-start(bf16[128,5376]{1,0:T(8,128)(2,1)S(1)} %collective-permute-done.2.refs_5_) | copy-start | bytes 4128772
  80.5 7.6 %collective-permute-start.4 = (bf16[128,5376]{1,0:T(8,128)(2,1)S(1)}, bf16[128,5376]{1,0:T(8,128)(2,1)}, u32[]{:S(2)}, u32[]{:S(2)}) collective-permute-start(bf16[128,5376]{1,0:T(8,128)(2,1)S(1)} %collective-permute-done.2.refs_5_), channel_id=1, source_target_pairs={{0,1},{1,0},{2,3},{3,2},{4,5},{5,4},{6,7},{7,6},{8,9},{9,8},{10,11... | collective-permute-start | bytes 4128776 | tf_op jit(solution)/shard_map/ppermute | solution.py:302
  85.2 5.4 %collective-permute-start.5 = (bf16[128,5376]{1,0:T(8,128)(2,1)}, bf16[128,5376]{1,0:T(8,128)(2,1)}, u32[]{:S(2)}, u32[]{:S(2)}) collective-permute-start(bf16[128,5376]{1,0:T(8,128)(2,1)} %collective-permute-done.3.refs_6_), channel_id=1, source_target_pairs={{0,1},{1,0},{2,3},{3,2},{4,5},{5,4},{6,7},{7,6},{8,9},{9,8},{10,11... | collective-permute-start | bytes 4128776 | tf_op jit(solution)/shard_map/ppermute | solution.py:302
Sparse Core Ops, SparseCore 0:
  43.8 53.0 all-gather.2

commit v3 on v2

--- a/solution.py
+++ b/solution.py
@@ -24,8 +24,8 @@
 
 
 def loss_kernel(*refs):
-    g_any, blocks = refs[0], refs[1:9]
-    gain_ref, target_ref, place_ref, out_ref, g, e, xn, logits, g_sem, e_sem = refs[9:]
+    g_any, blocks = refs[0], refs[1:5]
+    gain_ref, target_ref, place_ref, out_ref, g, e, xn, logits, g_sem, e_sem = refs[5:]
 
     def g_copy(pair):
         rows = pl.ds(pl.multiple_of(pair * PAIR_ROWS, PAIR_ROWS), PAIR_ROWS)
@@ -33,11 +33,10 @@
 
     for pair in range(PAIRS):
         g_copy(pair).start()
-    e_copies, first_row = [], 0
-    for i, block in enumerate(blocks):
-        words = slice(first_row, first_row + block.shape[0])
-        e_copies.append(pltpu.make_async_copy(block, e.at[words, :], e_sem.at[i]))
-        first_row += block.shape[0]
+    e_copies = [
+        pltpu.make_async_copy(block, e.at[i * VOCAB_LOCAL : (i + 1) * VOCAB_LOCAL, :], e_sem.at[i])
+        for i, block in enumerate(blocks)
+    ]
     for copy in e_copies:
         copy.start()
     lane = lax.broadcasted_iota(jnp.int32, (16, 128), 1)
@@ -81,7 +80,7 @@
 
     lax.fori_loop(0, PAIRS, pair_step, 0)
 
-    for words, arrivals in ((slice(0, WORDS // 2), e_copies[:4]), (slice(WORDS // 2, WORDS), e_copies[4:])):
+    for words, arrivals in ((slice(0, WORDS // 2), e_copies[:2]), (slice(WORDS // 2, WORDS), e_copies[2:])):
         for copy in arrivals:
             copy.wait()
         logits[:, words] = lax.dot_general(
@@ -115,11 +114,11 @@
     any_space = pl.BlockSpec(memory_space=pl.ANY)
     vmem = pl.BlockSpec(memory_space=pltpu.VMEM)
     gathered = pltpu.with_memory_space_constraint(gathered, pltpu.HBM)
-    blocks = [pltpu.with_memory_space_constraint(a, pltpu.HBM) for a in blocks]
+    blocks = [pltpu.with_memory_space_constraint(a, pltpu.VMEM) for a in blocks]
     return pl.pallas_call(
         loss_kernel,
         out_shape=jax.ShapeDtypeStruct((8, TOKENS), jnp.float32),
-        in_specs=[any_space] * 9 + [vmem, vmem, pl.BlockSpec(memory_space=pltpu.SMEM)],
+        in_specs=[any_space] * 5 + [vmem, vmem,  pl.BlockSpec(memory_space=pltpu.SMEM)],
         out_specs=vmem,
         scratch_shapes=[
             pltpu.VMEM((NY, PAIRS * PAIR_ROWS, 128), jnp.bfloat16),
@@ -129,7 +128,7 @@
             pltpu.SemaphoreType.DMA((PAIRS,)),
             pltpu.SemaphoreType.DMA((len(blocks),)),
         ],
-        compiler_params=pltpu.CompilerParams(vmem_limit_bytes=32 * 1024 * 1024),
+        compiler_params=pltpu.CompilerParams(vmem_limit_bytes=24 * 1024 * 1024),
         cost_estimate=pl.CostEstimate(flops=2 * TOKENS * WORDS * H, bytes_accessed=16 * 1024 * 1024, transcendentals=TOKENS * WORDS),
     )(gathered, *blocks, gain, target, place)
 
@@ -141,19 +140,23 @@
     for m in range(2):
         target = jnp.sum(jnp.where(row == column, targets_ref[m : m + 1, :], 0), axis=1, keepdims=True)
         digits = jnp.where(lane == 80, target & 127, jnp.where(lane == 81, (target >> 7) & 127, target >> 14))
+        first, second = (hidden_ref[m, :, k : k + 128].astype(jnp.float32) for k in (0, 128))
         tail = jnp.pad(hidden_ref[m, :, 256:336].astype(jnp.float32), ((0, 0), (0, 48)))
-        tail = jnp.where(lane < 80, tail, jnp.where(lane < 83, digits.astype(jnp.float32), 0.0))
-        tail = tail.astype(jnp.bfloat16)
-        for s in range(SOURCES):
-            out_ref[2 * s + m, :, 0:256] = hidden_ref[m, :, 0:256]
-            out_ref[2 * s + m, :, 256:384] = tail
+        tail = jnp.where(lane < 80, tail, digits.astype(jnp.float32))
+        fold = jnp.concatenate([pltpu.roll(tail[16:24], 83, 1), pltpu.roll(tail[16:24], 41, 1)], axis=0)
+        parts = [first[0:16], second[0:16], jnp.concatenate([first[16:24], second[16:24]], axis=0)]
+        parts.append(jnp.where(lane[0:16] < 83, tail[0:16], fold))
+        for i, part in enumerate(parts):
+            part = part.astype(jnp.bfloat16)
+            for s in range(SOURCES):
+                out_ref[2 * s + m, i * 16 : (i + 1) * 16, :] = part
 
 
 def prepare(hidden, targets):
     hidden, targets = (pltpu.with_memory_space_constraint(a, pltpu.HBM) for a in (hidden, targets))
     return pl.pallas_call(
         prepare_kernel,
-        out_shape=pltpu.HBM((2 * SOURCES, 24, 384), jnp.bfloat16),
+        out_shape=jax.ShapeDtypeStruct((2 * SOURCES, 64, 128), jnp.bfloat16),
         compiler_params=SMALL,
     )(hidden, targets)
 
@@ -164,12 +167,19 @@
     weight = jnp.where(lane == 80, 1, jnp.where(lane == 81, 128, jnp.where(lane == 82, 16384, 0))).astype(jnp.float32)
 
     def pair_step(pair, carry):
-        def tile(c, j):
-            both = [got_ref[4 * pair + 2 * d + c, :, j * 128 : (j + 1) * 128].astype(jnp.float32) for d in range(2)]
-            return jnp.concatenate(both, axis=0)
-
-        a, b = tile(0, 2), tile(1, 2)
-        tiles = [tile(0, 0), tile(0, 1), tile(1, 0), tile(1, 1), jnp.where(lane < 80, a, pltpu.roll(b, 80, 1))]
+        def rows_of(c):
+            whole, tails = ([], []), []
+            for d in range(2):
+                block = [got_ref[4 * pair + 2 * d + c, i * 16 : (i + 1) * 16, :].astype(jnp.float32) for i in range(4)]
+                whole[0].extend([block[0], block[2][0:8]])
+                whole[1].extend([block[1], block[2][8:16]])
+                fold = block[3]
+                unfolded = jnp.where(short[0:8] < 42, pltpu.roll(fold[0:8], 45, 1), pltpu.roll(fold[8:16], 87, 1))
+                tails.extend([fold, unfolded])
+            return [jnp.concatenate(part, axis=0) for part in (*whole, tails)]
+
+        (a0, a1, a), (b0, b1, b) = rows_of(0), rows_of(1)
+        tiles = [a0, a1, b0, b1, jnp.where(lane < 80, a, pltpu.roll(b, 80, 1))]
         base = pair * PAIR_ROWS
         for j in range(5):
             rows = pl.ds(pl.multiple_of(base + j * 48, 16), 48)
@@ -242,16 +252,17 @@
     )(gain.reshape(1, H))
 
 
-def reorder_kernel(ref, *out_refs):
+def reorder_kernel(ref, out_ref, *piece_refs):
     lane = lax.broadcasted_iota(jnp.int32, (16, 128), 1)
-    for n, out_ref in enumerate(out_refs):
+    for n, piece_ref in enumerate(piece_refs):
 
         def step(i, carry):
             src = pl.ds(pl.multiple_of(n * PIECE + i * 16, 16), 16)
             dst = pl.ds(pl.multiple_of(i * 16, 16), 16)
             tiles = [ref[src, k * 128 : (k + 1) * 128].astype(jnp.float32) for k in range(H // 128)]
             for k, tile in enumerate(arrange(tiles, lane)):
-                out_ref[dst, k * 128 : (k + 1) * 128] = tile.astype(jnp.bfloat16)
+                columns = slice(k * 128, (k + 1) * 128)
+                out_ref[src, columns] = piece_ref[dst, columns] = tile.astype(jnp.bfloat16)
             return carry
 
         lax.fori_loop(0, PIECE // 16, step, 0)
@@ -261,7 +272,7 @@
     piece = jax.ShapeDtypeStruct((PIECE, H), jnp.bfloat16)
     return pl.pallas_call(
         reorder_kernel,
-        out_shape=(piece, piece),
+        out_shape=(jax.ShapeDtypeStruct((VOCAB_LOCAL, H), jnp.bfloat16), piece, piece),
         compiler_params=pltpu.CompilerParams(vmem_limit_bytes=16 * 1024 * 1024),
         cost_estimate=pl.CostEstimate(flops=VOCAB_LOCAL * H * 8, bytes_accessed=VOCAB_LOCAL * H * 4, transcendentals=0),
     )(rows)
@@ -294,13 +305,13 @@
     units, late, gain = tie((units, embedding, norm_gain))
     gathered = lax.all_gather(units, "y", axis=0)
 
-    low, high = reorder_rows(late)
+    own, low, high = reorder_rows(late)
     from_left = lax.ppermute(low, ("xh", "xl"), [(i, (i + 1) % 4) for i in range(4)])
     from_right = lax.ppermute(high, ("xh", "xl"), [(i, (i - 1) % 4) for i in range(4)])
-    near, far = [low, high], [from_left, from_right]
-    near += [lax.ppermute(rows, "core", swap) for rows in near]
-    far += [lax.ppermute(rows, "core", swap) for rows in far]
-    stats = local_losses(gathered, near + far, arrange_gain(gain), target, place)
+    beside = lax.ppermute(own, "core", swap)
+    far = jnp.concatenate([from_left, from_right], axis=0)
+    far_beside = lax.ppermute(far, "core", swap)
+    stats = local_losses(gathered, (own, beside, far, far_beside), arrange_gain(gain), target, place)
     stats = stats[:3].reshape(3, SOURCES, 24).transpose(1, 0, 2)
     stats = lax.all_to_all(stats, ("xh", "z"), 0, 0, tiled=True)
     part = jnp.stack(combine(stats[:, 0], stats[:, 1], stats[:, 2], 0))

time: 148 us -> 145 us (0.980)
  starting transfers between devices: 19.5 us -> 16.3 us
  local copies, waits for them, and re-layouts: 0.23 us -> 2.17 us
  Pallas kernels: 18.2 us -> 16.6 us
  blocking collectives: 65.8 us -> 64.3 us
    ppermute x4 -> x2, starting transfers between devices: 13 us -> 9.8 us  [the longest x1 5.22 us: per_device(): far_beside = lax.ppermute(far, 'core', swap)]
    all_gather x1, waiting for transfers between devices: 6.38 us -> 3.75 us  [per_device(): gathered = lax.all_gather(units, 'y', axis=0)]
    unnamed x6 -> x5, local copies, waits for them, and re-layouts: 0.01 us -> 1.87 us
    ppermute x4 -> x2, waiting for transfers between devices: 3.13 us -> 4.53 us  [the longest x1 4.53 us: per_device(): far_beside = lax.ppermute(far, 'core', swap)]
  transfers between devices with their start and end apart: 7 -> 5, of which waited for: 4 -> 4; matrix products, arithmetic and copies ran while one was open for 0% -> 0% of each run, Pallas kernels for 3% -> 3%
where the time goes in v3:
time: 145 us; the launch traced here: 144 us
  blocking collectives  64.3 us (44%)
  waiting for transfers between devices  30.7 us (21%)
  Pallas kernels  16.6 us (11%)
  starting transfers between devices  16.3 us (11%)
  between operations  13.6 us (9%)
  local copies, waits for them, and re-layouts  2.17 us (1%)
    all_to_all x1, blocking collectives, per_device(): got = lax.all_to_all(payload, ('xh', 'z', 'core'), 0, 0, tiled=True)  32.3 us
    ppermute x1, waiting for transfers between devices, per_device(): lax.ppermute(low, ('xh', 'xl'), [(i, (i + 1) % 4) for i in range(4)])  21.7 us
    all_to_all x1, blocking collectives, per_device(): stats = lax.all_to_all(stats, ('xh', 'z'), 0, 0, tiled=True)  18.3 us
    all_to_all x1, blocking collectives, per_device(): lax.all_to_all(jnp.broadcast_to(part[None], (16, 3, 24)), ('y', 'core'),...  13.8 us
    pallas_call x1, Pallas kernels, local_losses(): pl.pallas_call(loss_kernel, out_shape=jax.ShapeDtypeStruct((8, TOKENS), j...  9.6 us
    ppermute x1, starting transfers between devices, per_device(): far_beside = lax.ppermute(far, 'core', swap)  5.22 us
    ppermute x1, starting transfers between devices, per_device(): beside = lax.ppermute(own, 'core', swap)  4.58 us
    ppermute x1, waiting for transfers between devices, per_device(): far_beside = lax.ppermute(far, 'core', swap)  4.53 us
  transfers between devices with their start and end apart: 5, of which 4 were waited for; matrix products, arithmetic and copies ran while one was open for 0% of the time, Pallas kernels for 3%

profile of v3, /device:TPU:1, one launch (start us, length us, event | category | flops | bytes accessed | tf_op | source)
XLA Modules:
  0.0 144.3 jit_solution(3221557119248725219)
XLA Ops:
  6.5 0.0 all-gather.3.cloned.1.call-start
  6.5 0.9 shard_map.46
  7.5 32.3 %all_to_all.15.got_ref = bf16[32,64,128]{2,1,0:T(8,128)(2,1)S(1)} all-to-all(bf16[32,64,128]{2,1,0:T(8,128)(2,1)S(1)} %shard_map.46), channel_id=1, replica_groups=mesh['xh'=2,'xl'=2,'z'=8,'y'=8,'core'=2] {'xh','z','core'}, dimensions={0} | all-to-all | bytes 1048576 | tf_op jit(solution)/shard_map/all_to_all | solution.py:302
  39.8 2.1 %shard_map.47 = (bf16[2048,128]{1,0:T(8,128)(2,1)}, s32[384,1]{1,0:T(8,128)S(1)}) custom-call(bf16[32,64,128]{2,1,0:T(8,128)(2,1)S(1)} %all_to_all.15.got_ref), custom_call_target="tpu_custom_call" | custom-call | flops 2000000 | bytes 1200000 | tf_op jit(solution)/shard_map/pallas_call | solution.py:198
  41.9 0.0 all-gather.3.cloned.1.call-update
  41.9 0.0 copy-start
  42.0 1.8 %copy-done = bf16[256,5376]{1,0:T(8,128)(2,1)S(1)} copy-done((bf16[256,5376]{1,0:T(8,128)(2,1)S(1)}, bf16[256,5376]{1,0:T(8,128)(2,1)}, u32[]{:S(2)}) %copy-start) | copy-done | bytes 2752536
  43.7 3.8 %shard_map.48 = (bf16[256,5376]{1,0:T(8,128)(2,1)}, bf16[128,5376]{1,0:T(8,128)(2,1)S(1)}, bf16[128,5376]{1,0:T(8,128)(2,1)S(1)}) custom-call(bf16[256,5376]{1,0:T(8,128)(2,1)S(1)} %copy-done), custom_call_target="tpu_custom_call" | custom-call | flops 11010048 | bytes 5505024 | tf_op jit(solution)/shard_map/pallas_call | solution.py:273
  47.5 2.2 %collective-permute-start.1 = (bf16[128,5376]{1,0:T(8,128)(2,1)S(1)}, bf16[128,5376]{1,0:T(8,128)(2,1)S(1)}, u32[]{:S(2)}, u32[]{:S(2)}) collective-permute-start(bf16[128,5376]{1,0:T(8,128)(2,1)S(1)} %get-tuple-element.21), channel_id=1, source_target_pairs={{0,128},{128,256},{256,384},{384,0},{1,129},{129,257},{257,385},{3... | collective-permute-start | bytes 4128776 | tf_op jit(solution)/shard_map/ppermute | solution.py:309
  49.7 4.3 %collective-permute-start.2 = (bf16[128,5376]{1,0:T(8,128)(2,1)S(1)}, bf16[128,5376]{1,0:T(8,128)(2,1)S(1)}, u32[]{:S(2)}, u32[]{:S(2)}) collective-permute-start(bf16[128,5376]{1,0:T(8,128)(2,1)S(1)} %get-tuple-element.22), channel_id=1, source_target_pairs={{0,384},{128,0},{256,128},{384,256},{1,385},{129,1},{257,129},{385... | collective-permute-start | bytes 4128776 | tf_op jit(solution)/shard_map/ppermute | solution.py:310
  54.0 0.0 copy-start.1
  54.0 4.6 %collective-permute-start = (bf16[256,5376]{1,0:T(8,128)(2,1)}, bf16[256,5376]{1,0:T(8,128)(2,1)}, u32[]{:S(2)}, u32[]{:S(2)}) collective-permute-start(bf16[256,5376]{1,0:T(8,128)(2,1)} %get-tuple-element.20.refs_1_), channel_id=1, source_target_pairs={{0,1},{1,0},{2,3},{3,2},{4,5},{5,4},{6,7},{7,6},{8,9},{9,8},{10,11... | collective-permute-start | bytes 8257544 | tf_op jit(solution)/shard_map/ppermute | solution.py:311
  58.6 21.7 %collective-permute-done.1 = bf16[128,5376]{1,0:T(8,128)(2,1)S(1)} collective-permute-done((bf16[128,5376]{1,0:T(8,128)(2,1)S(1)}, bf16[128,5376]{1,0:T(8,128)(2,1)S(1)}, u32[]{:S(2)}, u32[]{:S(2)}) %collective-permute-start.1) | collective-permute-done | bytes 1376288 | tf_op jit(solution)/shard_map/ppermute | solution.py:309
  80.3 0.1 constant_dynamic-update-slice_fusion.1
  80.3 0.7 collective-permute-done.2
  81.0 0.1 constant_dynamic-update-slice_fusion.refs_3_
  81.1 5.2 %collective-permute-start.3 = (bf16[256,5376]{1,0:T(8,128)(2,1)S(1)}, bf16[256,5376]{1,0:T(8,128)(2,1)}, u32[]{:S(2)}, u32[]{:S(2)}) collective-permute-start(bf16[256,5376]{1,0:T(8,128)(2,1)S(1)} %constant_dynamic-update-slice_fusion.refs_3_), channel_id=1, source_target_pairs={{0,1},{1,0},{2,3},{3,2},{4,5},{5,4},{6,7},{7,6},{8,9},{9,8},{10,11... | collective-permute-start | bytes 8257544 | tf_op jit(solution)/shard_map/ppermute | solution.py:313
  86.4 0.1 stack.47.refs_7_
  86.5 0.0 copy-done.1
  86.5 0.1 shard_map.49.refs_5_
  86.7 0.0 collective-permute-done.refs_2_
  86.7 4.5 %collective-permute-done.3.refs_4_ = bf16[256,5376]{1,0:T(8,128)(2,1)} collective-permute-done((bf16[256,5376]{1,0:T(8,128)(2,1)S(1)}, bf16[256,5376]{1,0:T(8,128)(2,1)}, u32[]{:S(2)}, u32[]{:S(2)}) %collective-permute-start.3) | collective-permute-done | bytes 2752544 | tf_op jit(solution)/shard_map/ppermute | solution.py:313
  91.2 3.7 %all-gather.3.cloned.1.call-done = bf16[16384,128]{1,0:T(8,128)(2,1)} async-done(((bf16[2048,128]{1,0:T(8,128)(2,1)}), bf16[16384,128]{1,0:T(8,128)(2,1)}) %all-gather.3.cloned.1.call-update) | async-done | bytes 4194320 | tf_op jit(solution)/shard_map/all_gather | solution.py:306
  95.0 9.6 %shard_map.50 = f32[8,384]{1,0:T(8,128)S(1)} custom-call(bf16[8,2048,128]{2,1,0:T(8,128)(2,1)} %bitcast.41, bf16[256,5376]{1,0:T(8,128)(2,1)} %get-tuple-element.20.refs_1_, bf16[256,5376]{1,0:T(8,128)(2,1)} %collective-permute-done.refs_2_, bf16[256,5376]{1,0:T(8,128)(2,1)S(1)} %constant_dynamic-update-slice_fusion.refs_3_, ...), custom_call_target="tpu_custom_call" | custom-call | flops 4227858432 | bytes 16777216 | tf_op jit(solution)/shard_map/pallas_call | solution.py:118
  104.6 0.1 reshape.13
  104.7 18.3 %all_to_all.16 = f32[16,3,24]{2,1,0:T(4,128)S(1)} all-to-all(f32[16,3,24]{2,1,0:T(4,128)S(1)} %bitcast.34), channel_id=1, replica_groups=mesh['xh'=2,'xl'=2,'z'=8,'y'=8,'core'=2] {'xh','z'}, dimensions={0} | all-to-all | bytes 9216 | tf_op jit(solution)/shard_map/all_to_all | solution.py:316
  123.1 13.8 %all_to_all.17 = f32[16,3,24]{2,1,0:T(4,128)S(1)} all-to-all(f32[16,3,24]{2,1,0:T(4,128)S(1)} %broadcast_in_dim.2), channel_id=1, replica_groups=mesh['xh'=2,'xl'=2,'z'=8,'y'=8,'core'=2] {'y','core'}, dimensions={0} | all-to-all | bytes 9216 | tf_op jit(solution)/shard_map/all_to_all | solution.py:318
  136.9 0.6 add_subtract_fusion
  (11 shorter events, 0.2 us)
Async XLA Ops:
  6.5 88.4 %all-gather.3.cloned.1.call-start = ((), (), s32[]{:S(2)}) async-start(), calls=%async_computation.3 | async-start | bytes 4718592 | tf_op jit(solution)/shard_map/all_gather | solution.py:306
  41.9 1.8 %copy-start = (bf16[256,5376]{1,0:T(8,128)(2,1)S(1)}, bf16[256,5376]{1,0:T(8,128)(2,1)}, u32[]{:S(2)}) copy-start(bf16[256,5376]{1,0:T(8,128)(2,1)} %ref) | copy-start | bytes 8257540
  47.5 32.8 %collective-permute-start.1 = (bf16[128,5376]{1,0:T(8,128)(2,1)S(1)}, bf16[128,5376]{1,0:T(8,128)(2,1)S(1)}, u32[]{:S(2)}, u32[]{:S(2)}) collective-permute-start(bf16[128,5376]{1,0:T(8,128)(2,1)S(1)} %get-tuple-element.21), channel_id=1, source_target_pairs={{0,128},{128,256},{256,384},{384,0},{1,129},{129,257},{257,385},{3... | collective-permute-start | bytes 4128776 | tf_op jit(solution)/shard_map/ppermute | solution.py:309
  49.7 31.3 %collective-permute-start.2 = (bf16[128,5376]{1,0:T(8,128)(2,1)S(1)}, bf16[128,5376]{1,0:T(8,128)(2,1)S(1)}, u32[]{:S(2)}, u32[]{:S(2)}) collective-permute-start(bf16[128,5376]{1,0:T(8,128)(2,1)S(1)} %get-tuple-element.22), channel_id=1, source_target_pairs={{0,384},{128,0},{256,128},{384,256},{1,385},{129,1},{257,129},{385... | collective-permute-start | bytes 4128776 | tf_op jit(solution)/shard_map/ppermute | solution.py:310
  54.0 32.5 %copy-start.1 = (f32[5376]{0:T(1024)S(1)}, f32[5376]{0:T(1024)}, u32[]{:S(2)}) copy-start(f32[5376]{0:T(1024)} %param.5) | copy-start | bytes 64516
  54.0 32.7 %collective-permute-start = (bf16[256,5376]{1,0:T(8,128)(2,1)}, bf16[256,5376]{1,0:T(8,128)(2,1)}, u32[]{:S(2)}, u32[]{:S(2)}) collective-permute-start(bf16[256,5376]{1,0:T(8,128)(2,1)} %get-tuple-element.20.refs_1_), channel_id=1, source_target_pairs={{0,1},{1,0},{2,3},{3,2},{4,5},{5,4},{6,7},{7,6},{8,9},{9,8},{10,11... | collective-permute-start | bytes 8257544 | tf_op jit(solution)/shard_map/ppermute | solution.py:311
  81.1 10.1 %collective-permute-start.3 = (bf16[256,5376]{1,0:T(8,128)(2,1)S(1)}, bf16[256,5376]{1,0:T(8,128)(2,1)}, u32[]{:S(2)}, u32[]{:S(2)}) collective-permute-start(bf16[256,5376]{1,0:T(8,128)(2,1)S(1)} %constant_dynamic-update-slice_fusion.refs_3_), channel_id=1, source_target_pairs={{0,1},{1,0},{2,3},{3,2},{4,5},{5,4},{6,7},{7,6},{8,9},{9,8},{10,11... | collective-permute-start | bytes 8257544 | tf_op jit(solution)/shard_map/ppermute | solution.py:313
Sparse Core Ops, SparseCore 0:
  42.1 52.8 all-gather.2

commit v4 on v3

--- a/solution.py
+++ b/solution.py
@@ -191,7 +191,7 @@
         target_ref[pl.ds(pl.multiple_of(pair * 48, 16), 48), :] = target.astype(jnp.int32)
         return carry
 
-    lax.fori_loop(0, PAIRS, pair_step, 0)
+    lax.fori_loop(0, PAIRS, pair_step, 0, unroll=True)
 
 
 def repack(got):

time: 145 us -> 144 us (level)
  no operation moved by 1% of the time
where the time goes in v4:
time: 144 us
  blocking collectives  64.3 us (45%)
  waiting for transfers between devices  30.7 us (21%)
  starting transfers between devices  16.3 us (11%)
  Pallas kernels  16 us (11%)
  between operations  13.6 us (9%)
  local copies, waits for them, and re-layouts  2.17 us (2%)
    all_to_all x1, blocking collectives, per_device(): got = lax.all_to_all(payload, ('xh', 'z', 'core'), 0, 0, tiled=True)  32.3 us
    ppermute x1, waiting for transfers between devices, per_device(): lax.ppermute(low, ('xh', 'xl'), [(i, (i + 1) % 4) for i in range(4)])  21.7 us
    all_to_all x1, blocking collectives, per_device(): stats = lax.all_to_all(stats, ('xh', 'z'), 0, 0, tiled=True)  18.3 us
    all_to_all x1, blocking collectives, per_device(): lax.all_to_all(jnp.broadcast_to(part[None], (16, 3, 24)), ('y', 'core'),...  13.8 us
    pallas_call x1, Pallas kernels, local_losses(): pl.pallas_call(loss_kernel, out_shape=jax.ShapeDtypeStruct((8, TOKENS), j...  9.6 us
    ppermute x1, starting transfers between devices, per_device(): far_beside = lax.ppermute(far, 'core', swap)  5.22 us
    ppermute x1, starting transfers between devices, per_device(): beside = lax.ppermute(own, 'core', swap)  4.58 us
    ppermute x1, waiting for transfers between devices, per_device(): far_beside = lax.ppermute(far, 'core', swap)  4.53 us
  transfers between devices with their start and end apart: 5, of which 4 were waited for; matrix products, arithmetic and copies ran while one was open for 0% of the time, Pallas kernels for 3%

profile of v4, /device:TPU:1, one launch (start us, length us, event | category | flops | bytes accessed | tf_op | source)
XLA Modules:
  0.0 143.7 jit_solution(9926803313469699876)
XLA Ops:
  6.5 0.0 all-gather.3.cloned.1.call-start
  6.5 0.9 shard_map.46
  7.5 32.3 %all_to_all.15.got_ref = bf16[32,64,128]{2,1,0:T(8,128)(2,1)S(1)} all-to-all(bf16[32,64,128]{2,1,0:T(8,128)(2,1)S(1)} %shard_map.46), channel_id=1, replica_groups=mesh['xh'=2,'xl'=2,'z'=8,'y'=8,'core'=2] {'xh','z','core'}, dimensions={0} | all-to-all | bytes 1048576 | tf_op jit(solution)/shard_map/all_to_all | solution.py:302
  39.8 1.6 %shard_map.47 = (bf16[2048,128]{1,0:T(8,128)(2,1)}, s32[384,1]{1,0:T(8,128)S(1)}) custom-call(bf16[32,64,128]{2,1,0:T(8,128)(2,1)S(1)} %all_to_all.15.got_ref), custom_call_target="tpu_custom_call" | custom-call | flops 2000000 | bytes 1200000 | tf_op jit(solution)/shard_map/pallas_call | solution.py:198
  41.3 0.0 all-gather.3.cloned.1.call-update
  41.4 0.0 copy-start
  41.4 1.8 %copy-done = bf16[256,5376]{1,0:T(8,128)(2,1)S(1)} copy-done((bf16[256,5376]{1,0:T(8,128)(2,1)S(1)}, bf16[256,5376]{1,0:T(8,128)(2,1)}, u32[]{:S(2)}) %copy-start) | copy-done | bytes 2752536
  43.2 3.8 %shard_map.48 = (bf16[256,5376]{1,0:T(8,128)(2,1)}, bf16[128,5376]{1,0:T(8,128)(2,1)S(1)}, bf16[128,5376]{1,0:T(8,128)(2,1)S(1)}) custom-call(bf16[256,5376]{1,0:T(8,128)(2,1)S(1)} %copy-done), custom_call_target="tpu_custom_call" | custom-call | flops 11010048 | bytes 5505024 | tf_op jit(solution)/shard_map/pallas_call | solution.py:273
  46.9 2.2 %collective-permute-start.1 = (bf16[128,5376]{1,0:T(8,128)(2,1)S(1)}, bf16[128,5376]{1,0:T(8,128)(2,1)S(1)}, u32[]{:S(2)}, u32[]{:S(2)}) collective-permute-start(bf16[128,5376]{1,0:T(8,128)(2,1)S(1)} %get-tuple-element.21), channel_id=1, source_target_pairs={{0,128},{128,256},{256,384},{384,0},{1,129},{129,257},{257,385},{3... | collective-permute-start | bytes 4128776 | tf_op jit(solution)/shard_map/ppermute | solution.py:309
  49.1 4.3 %collective-permute-start.2 = (bf16[128,5376]{1,0:T(8,128)(2,1)S(1)}, bf16[128,5376]{1,0:T(8,128)(2,1)S(1)}, u32[]{:S(2)}, u32[]{:S(2)}) collective-permute-start(bf16[128,5376]{1,0:T(8,128)(2,1)S(1)} %get-tuple-element.22), channel_id=1, source_target_pairs={{0,384},{128,0},{256,128},{384,256},{1,385},{129,1},{257,129},{385... | collective-permute-start | bytes 4128776 | tf_op jit(solution)/shard_map/ppermute | solution.py:310
  53.4 0.0 copy-start.1
  53.4 4.6 %collective-permute-start = (bf16[256,5376]{1,0:T(8,128)(2,1)}, bf16[256,5376]{1,0:T(8,128)(2,1)}, u32[]{:S(2)}, u32[]{:S(2)}) collective-permute-start(bf16[256,5376]{1,0:T(8,128)(2,1)} %get-tuple-element.20.refs_1_), channel_id=1, source_target_pairs={{0,1},{1,0},{2,3},{3,2},{4,5},{5,4},{6,7},{7,6},{8,9},{9,8},{10,11... | collective-permute-start | bytes 8257544 | tf_op jit(solution)/shard_map/ppermute | solution.py:311
  58.0 21.7 %collective-permute-done.1 = bf16[128,5376]{1,0:T(8,128)(2,1)S(1)} collective-permute-done((bf16[128,5376]{1,0:T(8,128)(2,1)S(1)}, bf16[128,5376]{1,0:T(8,128)(2,1)S(1)}, u32[]{:S(2)}, u32[]{:S(2)}) %collective-permute-start.1) | collective-permute-done | bytes 1376288 | tf_op jit(solution)/shard_map/ppermute | solution.py:309
  79.7 0.1 constant_dynamic-update-slice_fusion.1
  79.8 0.7 collective-permute-done.2
  80.5 0.1 constant_dynamic-update-slice_fusion.refs_3_
  80.6 5.2 %collective-permute-start.3 = (bf16[256,5376]{1,0:T(8,128)(2,1)S(1)}, bf16[256,5376]{1,0:T(8,128)(2,1)}, u32[]{:S(2)}, u32[]{:S(2)}) collective-permute-start(bf16[256,5376]{1,0:T(8,128)(2,1)S(1)} %constant_dynamic-update-slice_fusion.refs_3_), channel_id=1, source_target_pairs={{0,1},{1,0},{2,3},{3,2},{4,5},{5,4},{6,7},{7,6},{8,9},{9,8},{10,11... | collective-permute-start | bytes 8257544 | tf_op jit(solution)/shard_map/ppermute | solution.py:313
  85.9 0.1 stack.47.refs_7_
  85.9 0.0 copy-done.1
  86.0 0.1 shard_map.49.refs_5_
  86.1 0.0 collective-permute-done.refs_2_
  86.1 4.5 %collective-permute-done.3.refs_4_ = bf16[256,5376]{1,0:T(8,128)(2,1)} collective-permute-done((bf16[256,5376]{1,0:T(8,128)(2,1)S(1)}, bf16[256,5376]{1,0:T(8,128)(2,1)}, u32[]{:S(2)}, u32[]{:S(2)}) %collective-permute-start.3) | collective-permute-done | bytes 2752544 | tf_op jit(solution)/shard_map/ppermute | solution.py:313
  90.6 3.7 %all-gather.3.cloned.1.call-done = bf16[16384,128]{1,0:T(8,128)(2,1)} async-done(((bf16[2048,128]{1,0:T(8,128)(2,1)}), bf16[16384,128]{1,0:T(8,128)(2,1)}) %all-gather.3.cloned.1.call-update) | async-done | bytes 4194320 | tf_op jit(solution)/shard_map/all_gather | solution.py:306
  94.4 9.6 %shard_map.50 = f32[8,384]{1,0:T(8,128)S(1)} custom-call(bf16[8,2048,128]{2,1,0:T(8,128)(2,1)} %bitcast.41, bf16[256,5376]{1,0:T(8,128)(2,1)} %get-tuple-element.20.refs_1_, bf16[256,5376]{1,0:T(8,128)(2,1)} %collective-permute-done.refs_2_, bf16[256,5376]{1,0:T(8,128)(2,1)S(1)} %constant_dynamic-update-slice_fusion.refs_3_, ...), custom_call_target="tpu_custom_call" | custom-call | flops 4227858432 | bytes 16777216 | tf_op jit(solution)/shard_map/pallas_call | solution.py:118
  104.0 0.1 reshape.13
  104.1 18.3 %all_to_all.16 = f32[16,3,24]{2,1,0:T(4,128)S(1)} all-to-all(f32[16,3,24]{2,1,0:T(4,128)S(1)} %bitcast.34), channel_id=1, replica_groups=mesh['xh'=2,'xl'=2,'z'=8,'y'=8,'core'=2] {'xh','z'}, dimensions={0} | all-to-all | bytes 9216 | tf_op jit(solution)/shard_map/all_to_all | solution.py:316
  122.5 13.8 %all_to_all.17 = f32[16,3,24]{2,1,0:T(4,128)S(1)} all-to-all(f32[16,3,24]{2,1,0:T(4,128)S(1)} %broadcast_in_dim.2), channel_id=1, replica_groups=mesh['xh'=2,'xl'=2,'z'=8,'y'=8,'core'=2] {'y','core'}, dimensions={0} | all-to-all | bytes 9216 | tf_op jit(solution)/shard_map/all_to_all | solution.py:318
  136.3 0.6 add_subtract_fusion
  (11 shorter events, 0.2 us)
Async XLA Ops:
  6.5 87.9 %all-gather.3.cloned.1.call-start = ((), (), s32[]{:S(2)}) async-start(), calls=%async_computation.3 | async-start | bytes 4718592 | tf_op jit(solution)/shard_map/all_gather | solution.py:306
  41.4 1.8 %copy-start = (bf16[256,5376]{1,0:T(8,128)(2,1)S(1)}, bf16[256,5376]{1,0:T(8,128)(2,1)}, u32[]{:S(2)}) copy-start(bf16[256,5376]{1,0:T(8,128)(2,1)} %ref) | copy-start | bytes 8257540
  46.9 32.8 %collective-permute-start.1 = (bf16[128,5376]{1,0:T(8,128)(2,1)S(1)}, bf16[128,5376]{1,0:T(8,128)(2,1)S(1)}, u32[]{:S(2)}, u32[]{:S(2)}) collective-permute-start(bf16[128,5376]{1,0:T(8,128)(2,1)S(1)} %get-tuple-element.21), channel_id=1, source_target_pairs={{0,128},{128,256},{256,384},{384,0},{1,129},{129,257},{257,385},{3... | collective-permute-start | bytes 4128776 | tf_op jit(solution)/shard_map/ppermute | solution.py:309
  49.1 31.3 %collective-permute-start.2 = (bf16[128,5376]{1,0:T(8,128)(2,1)S(1)}, bf16[128,5376]{1,0:T(8,128)(2,1)S(1)}, u32[]{:S(2)}, u32[]{:S(2)}) collective-permute-start(bf16[128,5376]{1,0:T(8,128)(2,1)S(1)} %get-tuple-element.22), channel_id=1, source_target_pairs={{0,384},{128,0},{256,128},{384,256},{1,385},{129,1},{257,129},{385... | collective-permute-start | bytes 4128776 | tf_op jit(solution)/shard_map/ppermute | solution.py:310
  53.4 32.5 %copy-start.1 = (f32[5376]{0:T(1024)S(1)}, f32[5376]{0:T(1024)}, u32[]{:S(2)}) copy-start(f32[5376]{0:T(1024)} %param.5) | copy-start | bytes 64516
  53.4 32.7 %collective-permute-start = (bf16[256,5376]{1,0:T(8,128)(2,1)}, bf16[256,5376]{1,0:T(8,128)(2,1)}, u32[]{:S(2)}, u32[]{:S(2)}) collective-permute-start(bf16[256,5376]{1,0:T(8,128)(2,1)} %get-tuple-element.20.refs_1_), channel_id=1, source_target_pairs={{0,1},{1,0},{2,3},{3,2},{4,5},{5,4},{6,7},{7,6},{8,9},{9,8},{10,11... | collective-permute-start | bytes 8257544 | tf_op jit(solution)/shard_map/ppermute | solution.py:311
  80.6 10.1 %collective-permute-start.3 = (bf16[256,5376]{1,0:T(8,128)(2,1)S(1)}, bf16[256,5376]{1,0:T(8,128)(2,1)}, u32[]{:S(2)}, u32[]{:S(2)}) collective-permute-start(bf16[256,5376]{1,0:T(8,128)(2,1)S(1)} %constant_dynamic-update-slice_fusion.refs_3_), channel_id=1, source_target_pairs={{0,1},{1,0},{2,3},{3,2},{4,5},{5,4},{6,7},{7,6},{8,9},{9,8},{10,11... | collective-permute-start | bytes 8257544 | tf_op jit(solution)/shard_map/ppermute | solution.py:313
Sparse Core Ops, SparseCore 0:
  41.5 52.8 all-gather.2

commit v5 on v0

v5 whole, which is shorter than its diff:
```python
import jax
import jax.numpy as jnp
import numpy as np
from jax import lax
from jax.experimental import pallas as pl
from jax.experimental.pallas import tpu as pltpu
from jax.sharding import Mesh
from jax.sharding import PartitionSpec as P

epsilon = 1e-06
H = 5376
PART = 336
PARTS = H // PART
SOURCES = 16
TOKENS = SOURCES * 24
OWN = 48
VOCAB_LOCAL = 256
WORDS = 4 * VOCAB_LOCAL
SMALL = pltpu.CompilerParams(vmem_limit_bytes=8 * 1024 * 1024)
PIECE = VOCAB_LOCAL // 2


def loss_kernel(*refs):
    rows_any, blocks = refs[0], refs[1:5]
    target_ref, place_ref, out_ref, xn, e, logits, x_sem, e_sem = refs[5:]
    x_copies = []
    for n in range(TOKENS // 96):
        rows = slice(n * 96, (n + 1) * 96)
        x_copies.append(pltpu.make_async_copy(rows_any.at[rows, :], xn.at[rows, :], x_sem.at[n]))
    e_copies = []
    for i, block in enumerate(blocks):
        words = slice(i * VOCAB_LOCAL, (i + 1) * VOCAB_LOCAL)
        e_copies.append(pltpu.make_async_copy(block, e.at[words, :], e_sem.at[i]))
    for copy in x_copies + e_copies:
        copy.start()
    for words, arrivals in ((slice(0, WORDS // 2), x_copies + e_copies[:2]), (slice(WORDS // 2, WORDS), e_copies[2:])):
        for copy in arrivals:
            copy.wait()
        logits[:, words] = lax.dot_general(
            xn[...], e[words, :], (((1,), (1,)), ((), ())), preferred_element_type=jnp.float32
        )

    lane = lax.broadcasted_iota(jnp.int32, (48, 128), 1)
    stats = []
    for step in range(TOKENS // 48):
        rows = pl.ds(step * 48, 48)
        parts = [logits[rows, i * 128 : (i + 1) * 128] for i in range(WORDS // 128)]
        peak = parts[0]
        for part in parts[1:]:
            peak = jnp.maximum(peak, part)
        peak = jnp.max(peak, axis=1, keepdims=True)
        target = target_ref[rows, :]
        total = jnp.zeros((48, 128), jnp.float32)
        picked = jnp.zeros((48, 128), jnp.float32)
        for i, part in enumerate(parts):
            total = total + jnp.exp(part - peak)
            picked = picked + jnp.where(target - place_ref[i] == lane, part, 0.0)
        total = jnp.sum(total, axis=1, keepdims=True)
        picked = jnp.sum(picked, axis=1, keepdims=True)
        stats.append(jnp.where(lane == 0, peak, jnp.where(lane == 1, total, picked)))
    stats = jnp.concatenate(stats, axis=0)
    for i in range(TOKENS // 128):
        out_ref[:, i * 128 : (i + 1) * 128] = stats[i * 128 : (i + 1) * 128, :].T[0:8, :]


def local_losses(rows, blocks, target, place):
    any_space = pl.BlockSpec(memory_space=pl.ANY)
    vmem = pl.BlockSpec(memory_space=pltpu.VMEM)
    rows = pltpu.with_memory_space_constraint(rows, pltpu.HBM)
    blocks = [pltpu.with_memory_space_constraint(a, pltpu.VMEM) for a in blocks]
    return pl.pallas_call(
        loss_kernel,
        out_shape=jax.ShapeDtypeStruct((8, TOKENS), jnp.float32),
        in_specs=[any_space] * 5 + [vmem, pl.BlockSpec(memory_space=pltpu.SMEM)],
        out_specs=vmem,
        scratch_shapes=[
            pltpu.VMEM((TOKENS, H), jnp.bfloat16),
            pltpu.VMEM((WORDS, H), jnp.bfloat16),
            pltpu.VMEM((TOKENS, WORDS), jnp.float32),
            pltpu.SemaphoreType.DMA((TOKENS // 96,)),
            pltpu.SemaphoreType.DMA((len(blocks),)),
        ],
        compiler_params=pltpu.CompilerParams(vmem_limit_bytes=24 * 1024 * 1024),
        cost_estimate=pl.CostEstimate(flops=2 * TOKENS * WORDS * H, bytes_accessed=16 * 1024 * 1024, transcendentals=TOKENS * WORDS),
    )(rows, *blocks, target, place)


def prepare_kernel(hidden_ref, out_ref):
    lane = lax.broadcasted_iota(jnp.int32, (16, 128), 1)
    for m in range(2):
        first, second = (hidden_ref[m, :, k : k + 128].astype(jnp.float32) for k in (0, 128))
        tail = jnp.pad(hidden_ref[m, :, 256:336].astype(jnp.float32), ((0, 0), (0, 48)))
        fold = jnp.concatenate([pltpu.roll(tail[16:24], 80, 1), pltpu.roll(tail[16:24], 40, 1)], axis=0)
        parts = [first[0:16], second[0:16], jnp.concatenate([first[16:24], second[16:24]], axis=0)]
        parts.append(jnp.where(lane < 80, tail[0:16], fold))
        for i, part in enumerate(parts):
            part = part.astype(jnp.bfloat16)
            for s in range(SOURCES):
                out_ref[2 * s + m, i * 16 : (i + 1) * 16, :] = part


def prepare(hidden):
    return pl.pallas_call(
        prepare_kernel,
        out_shape=jax.ShapeDtypeStruct((2 * SOURCES, 64, 128), jnp.bfloat16),
        compiler_params=SMALL,
    )(pltpu.with_memory_space_constraint(hidden, pltpu.HBM))


def normalize_kernel(got_ref, gain_any, out_ref, rows_ref, gain_ref, gain_sem):
    gain_copy = pltpu.make_async_copy(gain_any, gain_ref, gain_sem)
    gain_copy.start()
    lane = lax.broadcasted_iota(jnp.int32, (24, 128), 1)
    scales = []
    for d in range(2):
        tiles = []
        for p in range(PARTS):
            block = [got_ref[d * PARTS + p, i * 16 : (i + 1) * 16, :].astype(jnp.float32) for i in range(4)]
            fold = block[3]
            unfolded = jnp.where(lane[0:8] < 40, pltpu.roll(fold[0:8], 48, 1), pltpu.roll(fold[8:16], 88, 1))
            whole = [(block[0], block[2][0:8]), (block[1], block[2][8:16]), (fold, unfolded)]
            tiles += [(p * PART + k * 128, jnp.concatenate(pair, axis=0)) for k, pair in enumerate(whole)]
        square = jnp.zeros((24, 128), jnp.float32)
        for t in range(H // 128):
            joined = None
            for begin, tile in tiles:
                width = 128 if begin % PART < 256 else 80
                at = begin - t * 128
                if at + width <= 0 or at >= 128:
                    continue
                moved = pltpu.roll(tile, at % 128, 1) if at % 128 else tile
                joined = moved if joined is None else jnp.where(lane >= at, moved, joined)
            rows_ref[d * 24 : (d + 1) * 24, t * 128 : (t + 1) * 128] = joined
            square = square + joined * joined
        scales.append(lax.rsqrt(jnp.sum(square, axis=1, keepdims=True) / H + epsilon))
    scale = jnp.concatenate(scales, axis=0)
    gain_copy.wait()
    for t in range(H // 128):
        columns = slice(t * 128, (t + 1) * 128)
        out_ref[:, columns] = (rows_ref[:, columns] * scale * gain_ref[columns].reshape(1, 128)).astype(jnp.bfloat16)


def normalize(got, gain):
    return pl.pallas_call(
        normalize_kernel,
        out_shape=pltpu.HBM((OWN, H), jnp.bfloat16),
        in_specs=[pl.BlockSpec(memory_space=pltpu.VMEM), pl.BlockSpec(memory_space=pl.ANY)],
        scratch_shapes=[pltpu.VMEM((OWN, H), jnp.float32), pltpu.VMEM((H,), jnp.float32), pltpu.SemaphoreType.DMA],
        compiler_params=SMALL,
        cost_estimate=pl.CostEstimate(flops=2000000, bytes_accessed=1200000, transcendentals=0),
    )(got, pltpu.with_memory_space_constraint(gain, pltpu.HBM))


def combine(peak, total, picked, axis):
    top = jnp.max(peak, axis=axis)
    total = jnp.sum(total * jnp.exp(peak - jnp.expand_dims(top, axis)), axis=axis)
    return top, total, jnp.sum(picked, axis=axis)


def per_device(hidden, norm_gain, embedding, targets):
    swap = [(0, 1), (1, 0)]
    tie = lax.optimization_barrier
    xh, xl, z, y, core = (lax.axis_index(a) for a in ("xh", "xl", "z", "y", "core"))

    x = xh * 2 + xl

    def first_row(at, c):
        return (((at % 4 * 8 + z) * 8 + y) * 2 + c) * VOCAB_LOCAL

    near = [first_row(x, c) + n * PIECE for c in (core, 1 - core) for n in range(2)]
    far = [first_row(x + 3 - 2 * n, c) + n * PIECE for c in (core, 1 - core) for n in range(2)]
    place = jnp.stack(near[:2] + far[:2] + near[2:] + far[2:])

    got = lax.all_to_all(prepare(hidden), ("xh", "y", "core"), 0, 0, tiled=True)
    normed = normalize(got, norm_gain)
    normed, late, asked = tie((normed, embedding, targets))
    rows = lax.all_gather(normed, "z", axis=0, tiled=True)

    from_left = lax.ppermute(late[:PIECE], ("xh", "xl"), [(i, (i + 1) % 4) for i in range(4)])
    from_right = lax.ppermute(late[PIECE:], ("xh", "xl"), [(i, (i - 1) % 4) for i in range(4)])
    beside = lax.ppermute(late, "core", swap)
    asked = jnp.broadcast_to(lax.dynamic_index_in_dim(asked, core, 0), (SOURCES, 24))
    target = lax.all_to_all(asked, ("z", "xh"), 0, 0, tiled=True).reshape(TOKENS, 1)
    from_left, from_right, target = tie((from_left, from_right, target))
    far = jnp.concatenate([from_left, from_right], axis=0)
    far_beside = lax.ppermute(far, "core", swap)
    stats = local_losses(rows, (late, far, beside, far_beside), target, place)
    stats = stats[:3].reshape(3, SOURCES, 24).transpose(1, 0, 2)
    stats = lax.all_to_all(stats, ("z", "xh"), 0, 0, tiled=True)
    part = jnp.stack(combine(stats[:, 0], stats[:, 1], stats[:, 2], 0))
    every = lax.all_to_all(jnp.broadcast_to(part[None], (16, 3, 24)), ("y", "core"), 0, 0, tiled=True)
    every = every.reshape(PARTS // 2, 2, 3, 24)
    peak, total, picked = combine(every[:, :, 0], every[:, :, 1], every[:, :, 2], 0)
    return peak + jnp.log(total) - picked


def solution(mesh):
    fine = Mesh(mesh.devices.reshape(2, 2, 8, 8, 2), ("xh", "xl", "z", "y", "core"))
    dp, pipe = ("xh", "xl", "z"), ("y", "core")
    placed = (P(None, dp, pipe), P(), P(dp + pipe, None), P(None, dp))
    return jax.shard_map(per_device, mesh=fine, in_specs=placed, out_specs=P(None, dp), check_vma=False)
```

time: 407 us -> 144 us (0.35)
  blocking collectives: 261 us -> 60.4 us
  waiting for transfers between devices: 104 us -> 22.3 us
  starting transfers between devices: 0.01 us -> 25.5 us
  Pallas kernels: 0 us -> 11.8 us
  other arithmetic: 11.9 us -> 1.39 us
  matrix products: 6.02 us -> 0 us
    all_gather x1, waiting for transfers between devices: 104 us -> 4.44 us  [per_device(): rows = lax.all_gather(normed, 'z', axis=0, tiled=True)]
    pmax x1 -> x0, blocking collectives: 95.8 us -> none  [per_device(): global_peak = lax.pmax(row_peak, ('dp', 'pipe'))]
    psum x1 -> x0, blocking collectives: 94.4 us -> none  [per_device(): global_total, global_pick = lax.psum((shifted, picked), ('dp', 'pipe'))]
    all_gather x2 -> x0, blocking collectives: 71 us -> none  [the longest x1 37.4 us: per_device(): piece_targets = lax.all_gather(targets, 'dp', axis=1, tiled=True)]
    all_to_all x0 -> x3, blocking collectives: none -> 60.4 us  [the longest x1 29.1 us: per_device(): got = lax.all_to_all(prepare(hidden), ('xh', 'y', 'core'), 0, 0, tiled=True)]
    ppermute x0 -> x4, starting transfers between devices: none -> 15 us  [the longest x1 5.15 us: per_device(): far_beside = lax.ppermute(far, 'core', swap)]
    all_to_all x0 -> x1, waiting for transfers between devices: none -> 13 us  [per_device(): lax.all_to_all(asked, ('z', 'xh'), 0, 0, tiled=True).reshape(TOKENS, 1)]
    pallas_call x0 -> x3, Pallas kernels: none -> 11.8 us  [the longest x1 8.74 us: local_losses(): pl.pallas_call(loss_kernel, out_shape=jax.ShapeDtypeStruct((8, TOKENS), j...]
  transfers between devices with their start and end apart: 1 -> 6, of which waited for: 1 -> 3; matrix products, arithmetic and copies ran while one was open for 0% -> 6% of each run, Pallas kernels for 0% -> 0%
where the time goes in v5:
time: 144 us; the launch traced here: 143 us
  blocking collectives  60.4 us (42%)
  starting transfers between devices  25.5 us (18%)
  waiting for transfers between devices  22.3 us (15%)
  between operations  13.6 us (9%)
  Pallas kernels  11.8 us (8%)
  local copies, waits for them, and re-layouts  8.45 us (6%)
    all_to_all x1, blocking collectives, per_device(): got = lax.all_to_all(prepare(hidden), ('xh', 'y', 'core'), 0, 0, tiled=True)  29.1 us
    all_to_all x1, blocking collectives, per_device(): stats = lax.all_to_all(stats, ('z', 'xh'), 0, 0, tiled=True)  16.8 us
    all_to_all x1, blocking collectives, per_device(): lax.all_to_all(jnp.broadcast_to(part[None], (16, 3, 24)), ('y', 'core'),...  14.6 us
    all_to_all x1, waiting for transfers between devices, per_device(): lax.all_to_all(asked, ('z', 'xh'), 0, 0, tiled=True).reshape(TOKENS, 1)  13 us
    all_to_all x1, starting transfers between devices, per_device(): lax.all_to_all(asked, ('z', 'xh'), 0, 0, tiled=True).reshape(TOKENS, 1)  10.5 us
    pallas_call x1, Pallas kernels, local_losses(): pl.pallas_call(loss_kernel, out_shape=jax.ShapeDtypeStruct((8, TOKENS), j...  8.74 us
    ppermute x1, starting transfers between devices, per_device(): far_beside = lax.ppermute(far, 'core', swap)  5.15 us
    ppermute x1, waiting for transfers between devices, per_device(): far_beside = lax.ppermute(far, 'core', swap)  4.75 us
  transfers between devices with their start and end apart: 6, of which 3 were waited for; matrix products, arithmetic and copies ran while one was open for 6% of the time, Pallas kernels for 0%

profile of v5, /device:TPU:1, one launch (start us, length us, event | category | flops | bytes accessed | tf_op | source)
XLA Modules:
  0.0 143.4 jit_solution(14676716793750812988)
XLA Ops:
  6.5 0.0 copy-start
  6.5 0.0 copy-start.1
  6.5 0.0 all-gather.2.cloned.1.call-start
  6.5 1.0 shard_map.46
  7.6 29.1 %all_to_all.21.got_ref = bf16[32,64,128]{2,1,0:T(8,128)(2,1)S(1)} all-to-all(bf16[32,64,128]{2,1,0:T(8,128)(2,1)S(1)} %shard_map.46), channel_id=1, replica_groups=mesh['xh'=2,'xl'=2,'z'=8,'y'=8,'core'=2] {'xh','y','core'}, dimensions={0} | all-to-all | bytes 1048576 | tf_op jit(solution)/shard_map/all_to_all | solution.py:174
  36.6 2.0 %shard_map.47 = bf16[48,5376]{1,0:T(8,128)(2,1)} custom-call(bf16[32,64,128]{2,1,0:T(8,128)(2,1)S(1)} %all_to_all.21.got_ref, f32[5376]{0:T(1024)} %gain_any.1), custom_call_target="tpu_custom_call" | custom-call | flops 2000000 | bytes 1200000 | tf_op jit(solution)/shard_map/pallas_call | solution.py:144
  38.7 0.0 all-gather.2.cloned.1.call-update
  38.7 0.0 copy-done.1
  38.7 1.7 %fusion.3 = (bf16[128,5376]{1,0:T(8,128)(2,1)}, bf16[128,5376]{1,0:T(8,128)(2,1)}) fusion(bf16[256,5376]{1,0:T(8,128)(2,1)S(1)} %copy-done.1), kind=kLoop, calls=%fused_computation.15 | loop fusion | bytes 5505024 | tf_op jit(solution)/shard_map/slice | solution.py:180
  40.5 2.0 %collective-permute-start.1 = (bf16[128,5376]{1,0:T(8,128)(2,1)}, bf16[128,5376]{1,0:T(8,128)(2,1)}, u32[]{:S(2)}, u32[]{:S(2)}) collective-permute-start(bf16[128,5376]{1,0:T(8,128)(2,1)} %get-tuple-element.19), channel_id=1, source_target_pairs={{0,384},{128,0},{256,128},{384,256},{1,385},{129,1},{257,129},{385... | collective-permute-start | bytes 4128776 | tf_op jit(solution)/shard_map/ppermute | solution.py:180
  42.5 3.2 %collective-permute-start = (bf16[128,5376]{1,0:T(8,128)(2,1)}, bf16[128,5376]{1,0:T(8,128)(2,1)}, u32[]{:S(2)}, u32[]{:S(2)}) collective-permute-start(bf16[128,5376]{1,0:T(8,128)(2,1)} %get-tuple-element.20), channel_id=1, source_target_pairs={{0,128},{128,256},{256,384},{384,0},{1,129},{129,257},{257,385},{3... | collective-permute-start | bytes 4128776 | tf_op jit(solution)/shard_map/ppermute | solution.py:179
  45.8 0.0 copy-done
  45.8 0.6 broadcast_in_dim.4
  46.4 10.5 %all-to-all-start.1 = ((s32[16,1,24]{2,1,0:T(1,128)}), s32[16,1,24]{2,1,0:T(1,128)S(1)}, u32[]{:S(2)}, u32[]{:S(2)}) async-start(s32[16,1,24]{2,1,0:T(1,128)} %broadcast_in_dim.4), calls=%async_computation.1 | async-start | bytes 16384 | tf_op jit(solution)/shard_map/all_to_all | solution.py:183
  56.9 4.6 %collective-permute-start.2 = (bf16[256,5376]{1,0:T(8,128)(2,1)S(1)}, bf16[256,5376]{1,0:T(8,128)(2,1)}, u32[]{:S(2)}, u32[]{:S(2)}) collective-permute-start(bf16[256,5376]{1,0:T(8,128)(2,1)S(1)} %copy-done.1), channel_id=1, source_target_pairs={{0,1},{1,0},{2,3},{3,2},{4,5},{5,4},{6,7},{7,6},{8,9},{9,8},{10,11... | collective-permute-start | bytes 8257544 | tf_op jit(solution)/shard_map/ppermute | solution.py:181
  61.5 13.0 %all-to-all-done.1 = s32[16,1,24]{2,1,0:T(1,128)S(1)} async-done(((s32[16,1,24]{2,1,0:T(1,128)}), s32[16,1,24]{2,1,0:T(1,128)S(1)}, u32[]{:S(2)}, u32[]{:S(2)}) %all-to-all-start.1) | async-done | bytes 1568 | tf_op jit(solution)/shard_map/all_to_all | solution.py:183
  74.5 0.5 broadcast.13
  75.0 0.7 reduce.7
  75.7 0.1 reshape.19
  75.8 0.0 collective-permute-done.1
  75.8 0.0 collective-permute-done
  75.8 2.6 %constant_dynamic-update-slice_fusion.1 = bf16[256,5376]{1,0:T(8,128)(2,1)} fusion(bf16[128,5376]{1,0:T(8,128)(2,1)} %collective-permute-done), kind=kLoop, calls=%fused_computation.11 | loop fusion | bytes 2752512
  78.4 2.6 %constant_dynamic-update-slice_fusion.refs_2_ = bf16[256,5376]{1,0:T(8,128)(2,1)} fusion(bf16[256,5376]{1,0:T(8,128)(2,1)} %constant_dynamic-update-slice_fusion.1, bf16[128,5376]{1,0:T(8,128)(2,1)} %collective-permute-done.1), kind=kLoop, calls=%fused_computation.10 | loop fusion | bytes 2752512 | tf_op jit(solution)/shard_map/concatenate | solution.py:185
  81.0 5.2 %collective-permute-start.3 = (bf16[256,5376]{1,0:T(8,128)(2,1)}, bf16[256,5376]{1,0:T(8,128)(2,1)}, u32[]{:S(2)}, u32[]{:S(2)}) collective-permute-start(bf16[256,5376]{1,0:T(8,128)(2,1)} %constant_dynamic-update-slice_fusion.refs_2_), channel_id=1, source_target_pairs={{0,1},{1,0},{2,3},{3,2},{4,5},{5,4},{6,7},{7,6},{8,9},{9,8},{10,11... | collective-permute-start | bytes 8257544 | tf_op jit(solution)/shard_map/ppermute | solution.py:186
  86.2 0.1 stack.47.refs_6_
  86.3 0.1 copy.23.refs_5_
  86.4 0.0 collective-permute-done.2.refs_3_
  86.4 4.7 %collective-permute-done.3.refs_4_ = bf16[256,5376]{1,0:T(8,128)(2,1)} collective-permute-done((bf16[256,5376]{1,0:T(8,128)(2,1)}, bf16[256,5376]{1,0:T(8,128)(2,1)}, u32[]{:S(2)}, u32[]{:S(2)}) %collective-permute-start.3) | collective-permute-done | bytes 2752544 | tf_op jit(solution)/shard_map/ppermute | solution.py:186
  91.2 4.4 %all-gather.2.cloned.1.call-done.refs_0_ = bf16[384,5376]{1,0:T(8,128)(2,1)} async-done(((bf16[48,5376]{1,0:T(8,128)(2,1)}), bf16[384,5376]{1,0:T(8,128)(2,1)}) %all-gather.2.cloned.1.call-update) | async-done | bytes 4128784 | tf_op jit(solution)/shard_map/all_gather | solution.py:177
  95.6 8.7 %shard_map.48 = f32[8,384]{1,0:T(8,128)S(1)} custom-call(bf16[384,5376]{1,0:T(8,128)(2,1)} %all-gather.2.cloned.1.call-done.refs_0_, bf16[256,5376]{1,0:T(8,128)(2,1)S(1)} %copy-done.1, bf16[256,5376]{1,0:T(8,128)(2,1)} %constant_dynamic-update-slice_fusion.refs_2_, bf16[256,5376]{1,0:T(8,128)(2,1)} %collective-permute-done.2.refs_3_, ...), custom_call_target="tpu_custom_call" | custom-call | flops 4227858432 | bytes 16777216 | tf_op jit(solution)/shard_map/pallas_call | solution.py:71
  104.4 0.1 reshape.20
  104.5 16.8 %all_to_all.22 = f32[16,3,24]{2,1,0:T(4,128)S(1)} all-to-all(f32[16,3,24]{2,1,0:T(4,128)S(1)} %bitcast.35), channel_id=1, replica_groups=mesh['xh'=2,'xl'=2,'z'=8,'y'=8,'core'=2] {'z','xh'}, dimensions={0} | all-to-all | bytes 9216 | tf_op jit(solution)/shard_map/all_to_all | solution.py:189
  121.4 14.6 %all_to_all.23 = f32[16,3,24]{2,1,0:T(4,128)S(1)} all-to-all(f32[16,3,24]{2,1,0:T(4,128)S(1)} %broadcast_in_dim.5), channel_id=1, replica_groups=mesh['xh'=2,'xl'=2,'z'=8,'y'=8,'core'=2] {'y','core'}, dimensions={0} | all-to-all | bytes 9216 | tf_op jit(solution)/shard_map/all_to_all | solution.py:191
  136.0 0.6 add_subtract_fusion
  (11 shorter events, 0.2 us)
Async XLA Ops:
  6.5 39.2 %copy-start = (s32[2,24]{1,0:T(2,128)S(1)}, s32[2,24]{1,0:T(2,128)}, u32[]{:S(2)}) copy-start(s32[2,24]{1,0:T(2,128)} %param.7) | copy-start | bytes 580
  6.5 32.2 %copy-start.1 = (bf16[256,5376]{1,0:T(8,128)(2,1)S(1)}, bf16[256,5376]{1,0:T(8,128)(2,1)}, u32[]{:S(2)}) copy-start(bf16[256,5376]{1,0:T(8,128)(2,1)} %refs_1_) | copy-start | bytes 8257540
  6.5 89.1 %all-gather.2.cloned.1.call-start = ((), (), s32[]{:S(2)}) async-start(), calls=%async_computation.4 | async-start | bytes 4644864 | tf_op jit(solution)/shard_map/all_gather | solution.py:177
  40.5 35.3 %collective-permute-start.1 = (bf16[128,5376]{1,0:T(8,128)(2,1)}, bf16[128,5376]{1,0:T(8,128)(2,1)}, u32[]{:S(2)}, u32[]{:S(2)}) collective-permute-start(bf16[128,5376]{1,0:T(8,128)(2,1)} %get-tuple-element.19), channel_id=1, source_target_pairs={{0,384},{128,0},{256,128},{384,256},{1,385},{129,1},{257,129},{385... | collective-permute-start | bytes 4128776 | tf_op jit(solution)/shard_map/ppermute | solution.py:180
  42.5 33.3 %collective-permute-start = (bf16[128,5376]{1,0:T(8,128)(2,1)}, bf16[128,5376]{1,0:T(8,128)(2,1)}, u32[]{:S(2)}, u32[]{:S(2)}) collective-permute-start(bf16[128,5376]{1,0:T(8,128)(2,1)} %get-tuple-element.20), channel_id=1, source_target_pairs={{0,128},{128,256},{256,384},{384,0},{1,129},{129,257},{257,385},{3... | collective-permute-start | bytes 4128776 | tf_op jit(solution)/shard_map/ppermute | solution.py:179
  46.4 28.1 %all-to-all-start.1 = ((s32[16,1,24]{2,1,0:T(1,128)}), s32[16,1,24]{2,1,0:T(1,128)S(1)}, u32[]{:S(2)}, u32[]{:S(2)}) async-start(s32[16,1,24]{2,1,0:T(1,128)} %broadcast_in_dim.4), calls=%async_computation.1 | async-start | bytes 16384 | tf_op jit(solution)/shard_map/all_to_all | solution.py:183
  56.9 29.5 %collective-permute-start.2 = (bf16[256,5376]{1,0:T(8,128)(2,1)S(1)}, bf16[256,5376]{1,0:T(8,128)(2,1)}, u32[]{:S(2)}, u32[]{:S(2)}) collective-permute-start(bf16[256,5376]{1,0:T(8,128)(2,1)S(1)} %copy-done.1), channel_id=1, source_target_pairs={{0,1},{1,0},{2,3},{3,2},{4,5},{5,4},{6,7},{7,6},{8,9},{9,8},{10,11... | collective-permute-start | bytes 8257544 | tf_op jit(solution)/shard_map/ppermute | solution.py:181
  81.0 10.2 %collective-permute-start.3 = (bf16[256,5376]{1,0:T(8,128)(2,1)}, bf16[256,5376]{1,0:T(8,128)(2,1)}, u32[]{:S(2)}, u32[]{:S(2)}) collective-permute-start(bf16[256,5376]{1,0:T(8,128)(2,1)} %constant_dynamic-update-slice_fusion.refs_2_), channel_id=1, source_target_pairs={{0,1},{1,0},{2,3},{3,2},{4,5},{5,4},{6,7},{7,6},{8,9},{9,8},{10,11... | collective-permute-start | bytes 8257544 | tf_op jit(solution)/shard_map/ppermute | solution.py:186
Sparse Core Ops, SparseCore 0:
  38.8 56.7 all-gather.1

commit v6 on v5

--- a/solution.py
+++ b/solution.py
@@ -21,19 +21,20 @@
 
 
 def loss_kernel(*refs):
-    rows_any, blocks = refs[0], refs[1:5]
-    target_ref, place_ref, out_ref, xn, e, logits, x_sem, e_sem = refs[5:]
+    rows_any, blocks = refs[0], refs[1:7]
+    target_ref, place_ref, out_ref, xn, e, logits, x_sem, e_sem = refs[7:]
     x_copies = []
     for n in range(TOKENS // 96):
         rows = slice(n * 96, (n + 1) * 96)
         x_copies.append(pltpu.make_async_copy(rows_any.at[rows, :], xn.at[rows, :], x_sem.at[n]))
-    e_copies = []
+    e_copies, begin = [], 0
     for i, block in enumerate(blocks):
-        words = slice(i * VOCAB_LOCAL, (i + 1) * VOCAB_LOCAL)
+        words = slice(begin, begin + block.shape[0])
+        begin += block.shape[0]
         e_copies.append(pltpu.make_async_copy(block, e.at[words, :], e_sem.at[i]))
     for copy in x_copies + e_copies:
         copy.start()
-    for words, arrivals in ((slice(0, WORDS // 2), x_copies + e_copies[:2]), (slice(WORDS // 2, WORDS), e_copies[2:])):
+    for words, arrivals in ((slice(0, WORDS // 2), x_copies + e_copies[:3]), (slice(WORDS // 2, WORDS), e_copies[3:])):
         for copy in arrivals:
             copy.wait()
         logits[:, words] = lax.dot_general(
@@ -71,7 +72,7 @@
     return pl.pallas_call(
         loss_kernel,
         out_shape=jax.ShapeDtypeStruct((8, TOKENS), jnp.float32),
-        in_specs=[any_space] * 5 + [vmem, pl.BlockSpec(memory_space=pltpu.SMEM)],
+        in_specs=[any_space] * 7 + [vmem, pl.BlockSpec(memory_space=pltpu.SMEM)],
         out_specs=vmem,
         scratch_shapes=[
             pltpu.VMEM((TOKENS, H), jnp.bfloat16),
@@ -85,7 +86,8 @@
     )(rows, *blocks, target, place)
 
 
-def prepare_kernel(hidden_ref, out_ref):
+def prepare_kernel(hidden_ref, gain_ref, out_ref, gain_out_ref):
+    gain_out_ref[...] = gain_ref[...]
     lane = lax.broadcasted_iota(jnp.int32, (16, 128), 1)
     for m in range(2):
         first, second = (hidden_ref[m, :, k : k + 128].astype(jnp.float32) for k in (0, 128))
@@ -99,17 +101,18 @@
                 out_ref[2 * s + m, i * 16 : (i + 1) * 16, :] = part
 
 
-def prepare(hidden):
+def prepare(hidden, gain):
     return pl.pallas_call(
         prepare_kernel,
-        out_shape=jax.ShapeDtypeStruct((2 * SOURCES, 64, 128), jnp.bfloat16),
+        out_shape=(
+            jax.ShapeDtypeStruct((2 * SOURCES, 64, 128), jnp.bfloat16),
+            jax.ShapeDtypeStruct((H,), jnp.float32),
+        ),
         compiler_params=SMALL,
-    )(pltpu.with_memory_space_constraint(hidden, pltpu.HBM))
-
-
-def normalize_kernel(got_ref, gain_any, out_ref, rows_ref, gain_ref, gain_sem):
-    gain_copy = pltpu.make_async_copy(gain_any, gain_ref, gain_sem)
-    gain_copy.start()
+    )(*(pltpu.with_memory_space_constraint(a, pltpu.HBM) for a in (hidden, gain)))
+
+
+def normalize_kernel(got_ref, gain_ref, out_ref, rows_ref):
     lane = lax.broadcasted_iota(jnp.int32, (24, 128), 1)
     scales = []
     for d in range(2):
@@ -134,7 +137,6 @@
             square = square + joined * joined
         scales.append(lax.rsqrt(jnp.sum(square, axis=1, keepdims=True) / H + epsilon))
     scale = jnp.concatenate(scales, axis=0)
-    gain_copy.wait()
     for t in range(H // 128):
         columns = slice(t * 128, (t + 1) * 128)
         out_ref[:, columns] = (rows_ref[:, columns] * scale * gain_ref[columns].reshape(1, 128)).astype(jnp.bfloat16)
@@ -144,11 +146,10 @@
     return pl.pallas_call(
         normalize_kernel,
         out_shape=pltpu.HBM((OWN, H), jnp.bfloat16),
-        in_specs=[pl.BlockSpec(memory_space=pltpu.VMEM), pl.BlockSpec(memory_space=pl.ANY)],
-        scratch_shapes=[pltpu.VMEM((OWN, H), jnp.float32), pltpu.VMEM((H,), jnp.float32), pltpu.SemaphoreType.DMA],
+        scratch_shapes=[pltpu.VMEM((OWN, H), jnp.float32)],
         compiler_params=SMALL,
         cost_estimate=pl.CostEstimate(flops=2000000, bytes_accessed=1200000, transcendentals=0),
-    )(got, pltpu.with_memory_space_constraint(gain, pltpu.HBM))
+    )(got, gain)
 
 
 def combine(peak, total, picked, axis):
@@ -171,8 +172,9 @@
     far = [first_row(x + 3 - 2 * n, c) + n * PIECE for c in (core, 1 - core) for n in range(2)]
     place = jnp.stack(near[:2] + far[:2] + near[2:] + far[2:])
 
-    got = lax.all_to_all(prepare(hidden), ("xh", "y", "core"), 0, 0, tiled=True)
-    normed = normalize(got, norm_gain)
+    payload, gain = prepare(hidden, norm_gain)
+    got = lax.all_to_all(payload, ("xh", "y", "core"), 0, 0, tiled=True)
+    normed = normalize(got, gain)
     normed, late, asked = tie((normed, embedding, targets))
     rows = lax.all_gather(normed, "z", axis=0, tiled=True)
 
@@ -182,9 +184,9 @@
     asked = jnp.broadcast_to(lax.dynamic_index_in_dim(asked, core, 0), (SOURCES, 24))
     target = lax.all_to_all(asked, ("z", "xh"), 0, 0, tiled=True).reshape(TOKENS, 1)
     from_left, from_right, target = tie((from_left, from_right, target))
-    far = jnp.concatenate([from_left, from_right], axis=0)
-    far_beside = lax.ppermute(far, "core", swap)
-    stats = local_losses(rows, (late, far, beside, far_beside), target, place)
+    far = [from_left, from_right]
+    far_beside = [lax.ppermute(part, "core", swap) for part in far]
+    stats = local_losses(rows, (late, *far, beside, *far_beside), target, place)
     stats = stats[:3].reshape(3, SOURCES, 24).transpose(1, 0, 2)
     stats = lax.all_to_all(stats, ("z", "xh"), 0, 0, tiled=True)
     part = jnp.stack(combine(stats[:, 0], stats[:, 1], stats[:, 2], 0))

time: 144 us -> 143 us (level)
  blocking collectives: 60.4 us -> 84.6 us
  waiting for transfers between devices: 22.3 us -> 10.6 us
  starting transfers between devices: 25.5 us -> 16.9 us
  local copies, waits for them, and re-layouts: 8.45 us -> 4.54 us
    all_to_all x1 -> x2, blocking collectives: 29.1 us -> 53.2 us  [the longest x1 29.1 us: per_device(): got = lax.all_to_all(payload, ('xh', 'y', 'core'), 0, 0, tiled=True)]
    all_to_all x1 -> x0, waiting for transfers between devices: 13 us -> none  [per_device(): lax.all_to_all(asked, ('z', 'xh'), 0, 0, tiled=True).reshape(TOKENS, 1)]
    all_to_all x1 -> x0, starting transfers between devices: 10.5 us -> none  [per_device(): lax.all_to_all(asked, ('z', 'xh'), 0, 0, tiled=True).reshape(TOKENS, 1)]
    all_gather x1, waiting for transfers between devices: 4.44 us -> 7.42 us  [per_device(): rows = lax.all_gather(normed, 'z', axis=0, tiled=True)]
    unnamed x5 -> x4, local copies, waits for them, and re-layouts: 2.61 us -> 0.01 us
    concatenate x1 -> x0, local copies, waits for them, and re-layouts: 2.55 us -> none  [per_device(): far = jnp.concatenate([from_left, from_right], axis=0)]
    ppermute x1 -> x2, starting transfers between devices: 5.15 us -> 7.09 us  [per_device(): far_beside = [lax.ppermute(part, 'core', swap) for part in far]]
    slice x1, local copies, waits for them, and re-layouts: 1.75 us -> 3.58 us  [per_device(): late[PIECE:]]
  transfers between devices with their start and end apart: 6 -> 6, of which waited for: 3 -> 3; matrix products, arithmetic and copies ran while one was open for 6% -> 4% of each run, Pallas kernels for 0% -> 0%
where the time goes in v6:
time: 143 us
  blocking collectives  84.6 us (59%)
  starting transfers between devices  16.9 us (12%)
  between operations  13.6 us (10%)
  Pallas kernels  11 us (8%)
  waiting for transfers between devices  10.6 us (7%)
  local copies, waits for them, and re-layouts  4.54 us (3%)
    all_to_all x1, blocking collectives, per_device(): got = lax.all_to_all(payload, ('xh', 'y', 'core'), 0, 0, tiled=True)  29.1 us
    all_to_all x1, blocking collectives, per_device(): lax.all_to_all(asked, ('z', 'xh'), 0, 0, tiled=True).reshape(TOKENS, 1)  24.1 us
    all_to_all x1, blocking collectives, per_device(): lax.all_to_all(jnp.broadcast_to(part[None], (16, 3, 24)), ('y', 'core'),...  16 us
    all_to_all x1, blocking collectives, per_device(): stats = lax.all_to_all(stats, ('z', 'xh'), 0, 0, tiled=True)  15.3 us
    pallas_call x1, Pallas kernels, local_losses(): pl.pallas_call(loss_kernel, out_shape=jax.ShapeDtypeStruct((8, TOKENS), j...  8.71 us
    all_gather x1, waiting for transfers between devices, per_device(): rows = lax.all_gather(normed, 'z', axis=0, tiled=True)  7.42 us
    ppermute x2, starting transfers between devices, per_device(): far_beside = [lax.ppermute(part, 'core', swap) for part in far]  7.09 us
    ppermute x1, starting transfers between devices, per_device(): beside = lax.ppermute(late, 'core', swap)  4.58 us
  transfers between devices with their start and end apart: 6, of which 3 were waited for; matrix products, arithmetic and copies ran while one was open for 4% of the time, Pallas kernels for 0%

profile of v6, /device:TPU:1, one launch (start us, length us, event | category | flops | bytes accessed | tf_op | source)
XLA Modules:
  0.0 142.6 jit_solution(6753925009069085549)
XLA Ops:
  6.5 0.0 copy-start
  6.5 0.0 all-gather.2.cloned.1.call-start
  6.5 0.9 shard_map.46
  7.4 29.1 %all_to_all.21.got_ref = bf16[32,64,128]{2,1,0:T(8,128)(2,1)S(1)} all-to-all(bf16[32,64,128]{2,1,0:T(8,128)(2,1)S(1)} %get-tuple-element.13), channel_id=1, replica_groups=mesh['xh'=2,'xl'=2,'z'=8,'y'=8,'core'=2] {'xh','y','core'}, dimensions={0} | all-to-all | bytes 1048576 | tf_op jit(solution)/shard_map/all_to_all | solution.py:176
  36.5 1.4 shard_map.47
  37.9 0.0 all-gather.2.cloned.1.call-update
  38.0 0.0 copy-start.1
  38.0 3.6 %fusion.3 = (bf16[128,5376]{1,0:T(8,128)(2,1)}, bf16[128,5376]{1,0:T(8,128)(2,1)}) fusion(bf16[256,5376]{1,0:T(8,128)(2,1)} %refs_1_), kind=kLoop, calls=%fused_computation.13 | loop fusion | bytes 5505024 | tf_op jit(solution)/shard_map/slice | solution.py:182
  41.5 2.0 %collective-permute-start.1 = (bf16[128,5376]{1,0:T(8,128)(2,1)}, bf16[128,5376]{1,0:T(8,128)(2,1)}, u32[]{:S(2)}, u32[]{:S(2)}) collective-permute-start(bf16[128,5376]{1,0:T(8,128)(2,1)} %get-tuple-element.23), channel_id=1, source_target_pairs={{0,384},{128,0},{256,128},{384,256},{1,385},{129,1},{257,129},{385... | collective-permute-start | bytes 4128776 | tf_op jit(solution)/shard_map/ppermute | solution.py:182
  43.6 3.2 %collective-permute-start = (bf16[128,5376]{1,0:T(8,128)(2,1)}, bf16[128,5376]{1,0:T(8,128)(2,1)}, u32[]{:S(2)}, u32[]{:S(2)}) collective-permute-start(bf16[128,5376]{1,0:T(8,128)(2,1)} %get-tuple-element.24), channel_id=1, source_target_pairs={{0,128},{128,256},{256,384},{384,0},{1,129},{129,257},{257,385},{3... | collective-permute-start | bytes 4128776 | tf_op jit(solution)/shard_map/ppermute | solution.py:181
  46.8 0.0 copy-done.1
  46.8 4.6 %collective-permute-start.2 = (bf16[256,5376]{1,0:T(8,128)(2,1)S(1)}, bf16[256,5376]{1,0:T(8,128)(2,1)}, u32[]{:S(2)}, u32[]{:S(2)}) collective-permute-start(bf16[256,5376]{1,0:T(8,128)(2,1)S(1)} %copy-done.1), channel_id=1, source_target_pairs={{0,1},{1,0},{2,3},{3,2},{4,5},{5,4},{6,7},{7,6},{8,9},{9,8},{10,11... | collective-permute-start | bytes 8257544 | tf_op jit(solution)/shard_map/ppermute | solution.py:183
  51.4 0.0 copy-done
  51.5 24.1 %all_to_all.22 = s32[16,1,24]{2,1,0:T(1,128)S(1)} all-to-all(s32[16,1,24]{2,1,0:T(1,128)S(1)} %broadcast_in_dim.4), channel_id=1, replica_groups=mesh['xh'=2,'xl'=2,'z'=8,'y'=8,'core'=2] {'z','xh'}, dimensions={0} | all-to-all | bytes 3072 | tf_op jit(solution)/shard_map/all_to_all | solution.py:185
  75.6 0.5 broadcast.13
  76.1 0.7 reduce.7
  76.8 0.1 reshape.19
  76.9 0.0 collective-permute-done.1.refs_3_
  76.9 0.0 collective-permute-done.refs_2_
  76.9 5.2 %collective-permute-start.3 = (bf16[128,5376]{1,0:T(8,128)(2,1)}, bf16[128,5376]{1,0:T(8,128)(2,1)}, u32[]{:S(2)}, u32[]{:S(2)}) collective-permute-start(bf16[128,5376]{1,0:T(8,128)(2,1)} %collective-permute-done.refs_2_), channel_id=1, source_target_pairs={{0,1},{1,0},{2,3},{3,2},{4,5},{5,4},{6,7},{7,6},{8,9},{9,8},{10,11... | collective-permute-start | bytes 4128776 | tf_op jit(solution)/shard_map/ppermute | solution.py:188
  82.1 1.9 %collective-permute-start.4 = (bf16[128,5376]{1,0:T(8,128)(2,1)}, bf16[128,5376]{1,0:T(8,128)(2,1)}, u32[]{:S(2)}, u32[]{:S(2)}) collective-permute-start(bf16[128,5376]{1,0:T(8,128)(2,1)} %collective-permute-done.1.refs_3_), channel_id=1, source_target_pairs={{0,1},{1,0},{2,3},{3,2},{4,5},{5,4},{6,7},{7,6},{8,9},{9,8},{10,11... | collective-permute-start | bytes 4128776 | tf_op jit(solution)/shard_map/ppermute | solution.py:188
  84.1 0.1 stack.47.refs_8_
  84.1 0.1 copy.23.refs_7_
  84.3 0.9 collective-permute-done.3.refs_5_
  85.2 2.3 %collective-permute-done.4.refs_6_ = bf16[128,5376]{1,0:T(8,128)(2,1)} collective-permute-done((bf16[128,5376]{1,0:T(8,128)(2,1)}, bf16[128,5376]{1,0:T(8,128)(2,1)}, u32[]{:S(2)}, u32[]{:S(2)}) %collective-permute-start.4) | collective-permute-done | bytes 1376288 | tf_op jit(solution)/shard_map/ppermute | solution.py:188
  87.4 0.0 collective-permute-done.2.refs_4_
  87.4 7.4 %all-gather.2.cloned.1.call-done.refs_0_ = bf16[384,5376]{1,0:T(8,128)(2,1)} async-done(((bf16[48,5376]{1,0:T(8,128)(2,1)}), bf16[384,5376]{1,0:T(8,128)(2,1)}) %all-gather.2.cloned.1.call-update) | async-done | bytes 4128784 | tf_op jit(solution)/shard_map/all_gather | solution.py:179
  94.9 8.7 %shard_map.48 = f32[8,384]{1,0:T(8,128)S(1)} custom-call(bf16[384,5376]{1,0:T(8,128)(2,1)} %all-gather.2.cloned.1.call-done.refs_0_, bf16[256,5376]{1,0:T(8,128)(2,1)S(1)} %copy-done.1, bf16[128,5376]{1,0:T(8,128)(2,1)} %collective-permute-done.refs_2_, bf16[128,5376]{1,0:T(8,128)(2,1)} %collective-permute-done.1.refs_3_, ...), custom_call_target="tpu_custom_call" | custom-call | flops 4227858432 | bytes 16777216 | tf_op jit(solution)/shard_map/pallas_call | solution.py:72
  103.6 0.1 reshape.20
  103.7 15.3 %all_to_all.23 = f32[16,3,24]{2,1,0:T(4,128)S(1)} all-to-all(f32[16,3,24]{2,1,0:T(4,128)S(1)} %bitcast.35), channel_id=1, replica_groups=mesh['xh'=2,'xl'=2,'z'=8,'y'=8,'core'=2] {'z','xh'}, dimensions={0} | all-to-all | bytes 9216 | tf_op jit(solution)/shard_map/all_to_all | solution.py:191
  119.1 16.0 %all_to_all.24 = f32[16,3,24]{2,1,0:T(4,128)S(1)} all-to-all(f32[16,3,24]{2,1,0:T(4,128)S(1)} %broadcast_in_dim.5), channel_id=1, replica_groups=mesh['xh'=2,'xl'=2,'z'=8,'y'=8,'core'=2] {'y','core'}, dimensions={0} | all-to-all | bytes 9216 | tf_op jit(solution)/shard_map/all_to_all | solution.py:193
  135.2 0.6 add_subtract_fusion
  (12 shorter events, 0.2 us)
Async XLA Ops:
  6.5 44.9 %copy-start = (s32[2,24]{1,0:T(2,128)S(1)}, s32[2,24]{1,0:T(2,128)}, u32[]{:S(2)}) copy-start(s32[2,24]{1,0:T(2,128)} %param.7) | copy-start | bytes 580
  6.5 88.3 %all-gather.2.cloned.1.call-start = ((), (), s32[]{:S(2)}) async-start(), calls=%async_computation.4 | async-start | bytes 4644864 | tf_op jit(solution)/shard_map/all_gather | solution.py:179
  38.0 8.9 %copy-start.1 = (bf16[256,5376]{1,0:T(8,128)(2,1)S(1)}, bf16[256,5376]{1,0:T(8,128)(2,1)}, u32[]{:S(2)}) copy-start(bf16[256,5376]{1,0:T(8,128)(2,1)} %refs_1_) | copy-start | bytes 8257540
  41.5 35.3 %collective-permute-start.1 = (bf16[128,5376]{1,0:T(8,128)(2,1)}, bf16[128,5376]{1,0:T(8,128)(2,1)}, u32[]{:S(2)}, u32[]{:S(2)}) collective-permute-start(bf16[128,5376]{1,0:T(8,128)(2,1)} %get-tuple-element.23), channel_id=1, source_target_pairs={{0,384},{128,0},{256,128},{384,256},{1,385},{129,1},{257,129},{385... | collective-permute-start | bytes 4128776 | tf_op jit(solution)/shard_map/ppermute | solution.py:182
  43.6 33.3 %collective-permute-start = (bf16[128,5376]{1,0:T(8,128)(2,1)}, bf16[128,5376]{1,0:T(8,128)(2,1)}, u32[]{:S(2)}, u32[]{:S(2)}) collective-permute-start(bf16[128,5376]{1,0:T(8,128)(2,1)} %get-tuple-element.24), channel_id=1, source_target_pairs={{0,128},{128,256},{256,384},{384,0},{1,129},{129,257},{257,385},{3... | collective-permute-start | bytes 4128776 | tf_op jit(solution)/shard_map/ppermute | solution.py:181
  46.8 40.6 %collective-permute-start.2 = (bf16[256,5376]{1,0:T(8,128)(2,1)S(1)}, bf16[256,5376]{1,0:T(8,128)(2,1)}, u32[]{:S(2)}, u32[]{:S(2)}) collective-permute-start(bf16[256,5376]{1,0:T(8,128)(2,1)S(1)} %copy-done.1), channel_id=1, source_target_pairs={{0,1},{1,0},{2,3},{3,2},{4,5},{5,4},{6,7},{7,6},{8,9},{9,8},{10,11... | collective-permute-start | bytes 8257544 | tf_op jit(solution)/shard_map/ppermute | solution.py:183
  76.9 8.3 %collective-permute-start.3 = (bf16[128,5376]{1,0:T(8,128)(2,1)}, bf16[128,5376]{1,0:T(8,128)(2,1)}, u32[]{:S(2)}, u32[]{:S(2)}) collective-permute-start(bf16[128,5376]{1,0:T(8,128)(2,1)} %collective-permute-done.refs_2_), channel_id=1, source_target_pairs={{0,1},{1,0},{2,3},{3,2},{4,5},{5,4},{6,7},{7,6},{8,9},{9,8},{10,11... | collective-permute-start | bytes 4128776 | tf_op jit(solution)/shard_map/ppermute | solution.py:188
  82.1 5.4 %collective-permute-start.4 = (bf16[128,5376]{1,0:T(8,128)(2,1)}, bf16[128,5376]{1,0:T(8,128)(2,1)}, u32[]{:S(2)}, u32[]{:S(2)}) collective-permute-start(bf16[128,5376]{1,0:T(8,128)(2,1)} %collective-permute-done.1.refs_3_), channel_id=1, source_target_pairs={{0,1},{1,0},{2,3},{3,2},{4,5},{5,4},{6,7},{7,6},{8,9},{9,8},{10,11... | collective-permute-start | bytes 4128776 | tf_op jit(solution)/shard_map/ppermute | solution.py:188
Sparse Core Ops, SparseCore 0:
  38.1 56.7 all-gather.1

commit v7 on v6

--- a/solution.py
+++ b/solution.py
@@ -34,7 +34,7 @@
         e_copies.append(pltpu.make_async_copy(block, e.at[words, :], e_sem.at[i]))
     for copy in x_copies + e_copies:
         copy.start()
-    for words, arrivals in ((slice(0, WORDS // 2), x_copies + e_copies[:3]), (slice(WORDS // 2, WORDS), e_copies[3:])):
+    for words, arrivals in ((slice(0, WORDS), x_copies + e_copies),):
         for copy in arrivals:
             copy.wait()
         logits[:, words] = lax.dot_general(

time: 143 us -> 144 us (level)
  no operation moved by 1% of the time
where the time goes in v7:
time: 144 us
  blocking collectives  84.6 us (59%)
  starting transfers between devices  16.9 us (12%)
  between operations  13.6 us (9%)
  Pallas kernels  12.4 us (9%)
  waiting for transfers between devices  10.6 us (7%)
  local copies, waits for them, and re-layouts  4.54 us (3%)
    all_to_all x1, blocking collectives, per_device(): got = lax.all_to_all(payload, ('xh', 'y', 'core'), 0, 0, tiled=True)  29.1 us
    all_to_all x1, blocking collectives, per_device(): lax.all_to_all(asked, ('z', 'xh'), 0, 0, tiled=True).reshape(TOKENS, 1)  24.1 us
    all_to_all x1, blocking collectives, per_device(): lax.all_to_all(jnp.broadcast_to(part[None], (16, 3, 24)), ('y', 'core'),...  16 us
    all_to_all x1, blocking collectives, per_device(): stats = lax.all_to_all(stats, ('z', 'xh'), 0, 0, tiled=True)  15.3 us
    pallas_call x1, Pallas kernels, local_losses(): pl.pallas_call(loss_kernel, out_shape=jax.ShapeDtypeStruct((8, TOKENS), j...  10.1 us
    all_gather x1, waiting for transfers between devices, per_device(): rows = lax.all_gather(normed, 'z', axis=0, tiled=True)  7.42 us
    ppermute x2, starting transfers between devices, per_device(): far_beside = [lax.ppermute(part, 'core', swap) for part in far]  7.09 us
    ppermute x1, starting transfers between devices, per_device(): beside = lax.ppermute(late, 'core', swap)  4.58 us
  transfers between devices with their start and end apart: 6, of which 3 were waited for; matrix products, arithmetic and copies ran while one was open for 4% of the time, Pallas kernels for 0%

profile of v7, /device:TPU:1, one launch (start us, length us, event | category | flops | bytes accessed | tf_op | source)
XLA Modules:
  0.0 144.0 jit_solution(6470173227808523514)
XLA Ops:
  6.5 0.0 copy-start
  6.5 0.0 all-gather.2.cloned.1.call-start
  6.5 0.9 shard_map.46
  7.4 29.1 %all_to_all.21.got_ref = bf16[32,64,128]{2,1,0:T(8,128)(2,1)S(1)} all-to-all(bf16[32,64,128]{2,1,0:T(8,128)(2,1)S(1)} %get-tuple-element.13), channel_id=1, replica_groups=mesh['xh'=2,'xl'=2,'z'=8,'y'=8,'core'=2] {'xh','y','core'}, dimensions={0} | all-to-all | bytes 1048576 | tf_op jit(solution)/shard_map/all_to_all | solution.py:176
  36.5 1.4 shard_map.47
  37.9 0.0 all-gather.2.cloned.1.call-update
  38.0 0.0 copy-start.1
  38.0 3.6 %fusion.3 = (bf16[128,5376]{1,0:T(8,128)(2,1)}, bf16[128,5376]{1,0:T(8,128)(2,1)}) fusion(bf16[256,5376]{1,0:T(8,128)(2,1)} %refs_1_), kind=kLoop, calls=%fused_computation.13 | loop fusion | bytes 5505024 | tf_op jit(solution)/shard_map/slice | solution.py:182
  41.5 2.0 %collective-permute-start.1 = (bf16[128,5376]{1,0:T(8,128)(2,1)}, bf16[128,5376]{1,0:T(8,128)(2,1)}, u32[]{:S(2)}, u32[]{:S(2)}) collective-permute-start(bf16[128,5376]{1,0:T(8,128)(2,1)} %get-tuple-element.23), channel_id=1, source_target_pairs={{0,384},{128,0},{256,128},{384,256},{1,385},{129,1},{257,129},{385... | collective-permute-start | bytes 4128776 | tf_op jit(solution)/shard_map/ppermute | solution.py:182
  43.6 3.2 %collective-permute-start = (bf16[128,5376]{1,0:T(8,128)(2,1)}, bf16[128,5376]{1,0:T(8,128)(2,1)}, u32[]{:S(2)}, u32[]{:S(2)}) collective-permute-start(bf16[128,5376]{1,0:T(8,128)(2,1)} %get-tuple-element.24), channel_id=1, source_target_pairs={{0,128},{128,256},{256,384},{384,0},{1,129},{129,257},{257,385},{3... | collective-permute-start | bytes 4128776 | tf_op jit(solution)/shard_map/ppermute | solution.py:181
  46.8 0.0 copy-done.1
  46.8 4.6 %collective-permute-start.2 = (bf16[256,5376]{1,0:T(8,128)(2,1)S(1)}, bf16[256,5376]{1,0:T(8,128)(2,1)}, u32[]{:S(2)}, u32[]{:S(2)}) collective-permute-start(bf16[256,5376]{1,0:T(8,128)(2,1)S(1)} %copy-done.1), channel_id=1, source_target_pairs={{0,1},{1,0},{2,3},{3,2},{4,5},{5,4},{6,7},{7,6},{8,9},{9,8},{10,11... | collective-permute-start | bytes 8257544 | tf_op jit(solution)/shard_map/ppermute | solution.py:183
  51.4 0.0 copy-done
  51.5 24.1 %all_to_all.22 = s32[16,1,24]{2,1,0:T(1,128)S(1)} all-to-all(s32[16,1,24]{2,1,0:T(1,128)S(1)} %broadcast_in_dim.4), channel_id=1, replica_groups=mesh['xh'=2,'xl'=2,'z'=8,'y'=8,'core'=2] {'z','xh'}, dimensions={0} | all-to-all | bytes 3072 | tf_op jit(solution)/shard_map/all_to_all | solution.py:185
  75.6 0.5 broadcast.13
  76.1 0.7 reduce.7
  76.8 0.1 reshape.19
  76.9 0.0 collective-permute-done.1.refs_3_
  76.9 0.0 collective-permute-done.refs_2_
  76.9 5.2 %collective-permute-start.3 = (bf16[128,5376]{1,0:T(8,128)(2,1)}, bf16[128,5376]{1,0:T(8,128)(2,1)}, u32[]{:S(2)}, u32[]{:S(2)}) collective-permute-start(bf16[128,5376]{1,0:T(8,128)(2,1)} %collective-permute-done.refs_2_), channel_id=1, source_target_pairs={{0,1},{1,0},{2,3},{3,2},{4,5},{5,4},{6,7},{7,6},{8,9},{9,8},{10,11... | collective-permute-start | bytes 4128776 | tf_op jit(solution)/shard_map/ppermute | solution.py:188
  82.1 1.9 %collective-permute-start.4 = (bf16[128,5376]{1,0:T(8,128)(2,1)}, bf16[128,5376]{1,0:T(8,128)(2,1)}, u32[]{:S(2)}, u32[]{:S(2)}) collective-permute-start(bf16[128,5376]{1,0:T(8,128)(2,1)} %collective-permute-done.1.refs_3_), channel_id=1, source_target_pairs={{0,1},{1,0},{2,3},{3,2},{4,5},{5,4},{6,7},{7,6},{8,9},{9,8},{10,11... | collective-permute-start | bytes 4128776 | tf_op jit(solution)/shard_map/ppermute | solution.py:188
  84.1 0.1 stack.47.refs_8_
  84.1 0.1 copy.23.refs_7_
  84.3 0.9 collective-permute-done.3.refs_5_
  85.2 2.3 %collective-permute-done.4.refs_6_ = bf16[128,5376]{1,0:T(8,128)(2,1)} collective-permute-done((bf16[128,5376]{1,0:T(8,128)(2,1)}, bf16[128,5376]{1,0:T(8,128)(2,1)}, u32[]{:S(2)}, u32[]{:S(2)}) %collective-permute-start.4) | collective-permute-done | bytes 1376288 | tf_op jit(solution)/shard_map/ppermute | solution.py:188
  87.4 0.0 collective-permute-done.2.refs_4_
  87.4 7.4 %all-gather.2.cloned.1.call-done.refs_0_ = bf16[384,5376]{1,0:T(8,128)(2,1)} async-done(((bf16[48,5376]{1,0:T(8,128)(2,1)}), bf16[384,5376]{1,0:T(8,128)(2,1)}) %all-gather.2.cloned.1.call-update) | async-done | bytes 4128784 | tf_op jit(solution)/shard_map/all_gather | solution.py:179
  94.9 10.1 %shard_map.48 = f32[8,384]{1,0:T(8,128)S(1)} custom-call(bf16[384,5376]{1,0:T(8,128)(2,1)} %all-gather.2.cloned.1.call-done.refs_0_, bf16[256,5376]{1,0:T(8,128)(2,1)S(1)} %copy-done.1, bf16[128,5376]{1,0:T(8,128)(2,1)} %collective-permute-done.refs_2_, bf16[128,5376]{1,0:T(8,128)(2,1)} %collective-permute-done.1.refs_3_, ...), custom_call_target="tpu_custom_call" | custom-call | flops 4227858432 | bytes 16777216 | tf_op jit(solution)/shard_map/pallas_call | solution.py:72
  105.0 0.1 reshape.20
  105.1 15.3 %all_to_all.23 = f32[16,3,24]{2,1,0:T(4,128)S(1)} all-to-all(f32[16,3,24]{2,1,0:T(4,128)S(1)} %bitcast.35), channel_id=1, replica_groups=mesh['xh'=2,'xl'=2,'z'=8,'y'=8,'core'=2] {'z','xh'}, dimensions={0} | all-to-all | bytes 9216 | tf_op jit(solution)/shard_map/all_to_all | solution.py:191
  120.5 16.0 %all_to_all.24 = f32[16,3,24]{2,1,0:T(4,128)S(1)} all-to-all(f32[16,3,24]{2,1,0:T(4,128)S(1)} %broadcast_in_dim.5), channel_id=1, replica_groups=mesh['xh'=2,'xl'=2,'z'=8,'y'=8,'core'=2] {'y','core'}, dimensions={0} | all-to-all | bytes 9216 | tf_op jit(solution)/shard_map/all_to_all | solution.py:193
  136.6 0.6 add_subtract_fusion
  (12 shorter events, 0.2 us)
Async XLA Ops:
  6.5 44.9 %copy-start = (s32[2,24]{1,0:T(2,128)S(1)}, s32[2,24]{1,0:T(2,128)}, u32[]{:S(2)}) copy-start(s32[2,24]{1,0:T(2,128)} %param.7) | copy-start | bytes 580
  6.5 88.3 %all-gather.2.cloned.1.call-start = ((), (), s32[]{:S(2)}) async-start(), calls=%async_computation.4 | async-start | bytes 4644864 | tf_op jit(solution)/shard_map/all_gather | solution.py:179
  38.0 8.9 %copy-start.1 = (bf16[256,5376]{1,0:T(8,128)(2,1)S(1)}, bf16[256,5376]{1,0:T(8,128)(2,1)}, u32[]{:S(2)}) copy-start(bf16[256,5376]{1,0:T(8,128)(2,1)} %refs_1_) | copy-start | bytes 8257540
  41.5 35.3 %collective-permute-start.1 = (bf16[128,5376]{1,0:T(8,128)(2,1)}, bf16[128,5376]{1,0:T(8,128)(2,1)}, u32[]{:S(2)}, u32[]{:S(2)}) collective-permute-start(bf16[128,5376]{1,0:T(8,128)(2,1)} %get-tuple-element.23), channel_id=1, source_target_pairs={{0,384},{128,0},{256,128},{384,256},{1,385},{129,1},{257,129},{385... | collective-permute-start | bytes 4128776 | tf_op jit(solution)/shard_map/ppermute | solution.py:182
  43.6 33.3 %collective-permute-start = (bf16[128,5376]{1,0:T(8,128)(2,1)}, bf16[128,5376]{1,0:T(8,128)(2,1)}, u32[]{:S(2)}, u32[]{:S(2)}) collective-permute-start(bf16[128,5376]{1,0:T(8,128)(2,1)} %get-tuple-element.24), channel_id=1, source_target_pairs={{0,128},{128,256},{256,384},{384,0},{1,129},{129,257},{257,385},{3... | collective-permute-start | bytes 4128776 | tf_op jit(solution)/shard_map/ppermute | solution.py:181
  46.8 40.6 %collective-permute-start.2 = (bf16[256,5376]{1,0:T(8,128)(2,1)S(1)}, bf16[256,5376]{1,0:T(8,128)(2,1)}, u32[]{:S(2)}, u32[]{:S(2)}) collective-permute-start(bf16[256,5376]{1,0:T(8,128)(2,1)S(1)} %copy-done.1), channel_id=1, source_target_pairs={{0,1},{1,0},{2,3},{3,2},{4,5},{5,4},{6,7},{7,6},{8,9},{9,8},{10,11... | collective-permute-start | bytes 8257544 | tf_op jit(solution)/shard_map/ppermute | solution.py:183
  76.9 8.3 %collective-permute-start.3 = (bf16[128,5376]{1,0:T(8,128)(2,1)}, bf16[128,5376]{1,0:T(8,128)(2,1)}, u32[]{:S(2)}, u32[]{:S(2)}) collective-permute-start(bf16[128,5376]{1,0:T(8,128)(2,1)} %collective-permute-done.refs_2_), channel_id=1, source_target_pairs={{0,1},{1,0},{2,3},{3,2},{4,5},{5,4},{6,7},{7,6},{8,9},{9,8},{10,11... | collective-permute-start | bytes 4128776 | tf_op jit(solution)/shard_map/ppermute | solution.py:188
  82.1 5.4 %collective-permute-start.4 = (bf16[128,5376]{1,0:T(8,128)(2,1)}, bf16[128,5376]{1,0:T(8,128)(2,1)}, u32[]{:S(2)}, u32[]{:S(2)}) collective-permute-start(bf16[128,5376]{1,0:T(8,128)(2,1)} %collective-permute-done.1.refs_3_), channel_id=1, source_target_pairs={{0,1},{1,0},{2,3},{3,2},{4,5},{5,4},{6,7},{7,6},{8,9},{9,8},{10,11... | collective-permute-start | bytes 4128776 | tf_op jit(solution)/shard_map/ppermute | solution.py:188
Sparse Core Ops, SparseCore 0:
  38.1 56.7 all-gather.1

commit v8 on v6

--- a/solution.py
+++ b/solution.py
@@ -112,7 +112,7 @@
     )(*(pltpu.with_memory_space_constraint(a, pltpu.HBM) for a in (hidden, gain)))
 
 
-def normalize_kernel(got_ref, gain_ref, out_ref, rows_ref):
+def normalize_kernel(got_ref, gain_ref, out_any, rows_ref, out_ref, out_sem):
     lane = lax.broadcasted_iota(jnp.int32, (24, 128), 1)
     scales = []
     for d in range(2):
@@ -137,16 +137,28 @@
             square = square + joined * joined
         scales.append(lax.rsqrt(jnp.sum(square, axis=1, keepdims=True) / H + epsilon))
     scale = jnp.concatenate(scales, axis=0)
-    for t in range(H // 128):
-        columns = slice(t * 128, (t + 1) * 128)
-        out_ref[:, columns] = (rows_ref[:, columns] * scale * gain_ref[columns].reshape(1, 128)).astype(jnp.bfloat16)
+    copies = []
+    for group in range(3):
+        for t in range(group * 14, group * 14 + 14):
+            columns = slice(t * 128, (t + 1) * 128)
+            out_ref[:, columns] = (rows_ref[:, columns] * scale * gain_ref[columns].reshape(1, 128)).astype(jnp.bfloat16)
+        done = slice(group * 1792, (group + 1) * 1792)
+        copies.append(pltpu.make_async_copy(out_ref.at[:, done], out_any.at[:, done], out_sem.at[group]))
+        copies[-1].start()
+    for copy in copies:
+        copy.wait()
 
 
 def normalize(got, gain):
     return pl.pallas_call(
         normalize_kernel,
         out_shape=pltpu.HBM((OWN, H), jnp.bfloat16),
-        scratch_shapes=[pltpu.VMEM((OWN, H), jnp.float32)],
+        out_specs=pl.BlockSpec(memory_space=pl.ANY),
+        scratch_shapes=[
+            pltpu.VMEM((OWN, H), jnp.float32),
+            pltpu.VMEM((OWN, H), jnp.bfloat16),
+            pltpu.SemaphoreType.DMA((3,)),
+        ],
         compiler_params=SMALL,
         cost_estimate=pl.CostEstimate(flops=2000000, bytes_accessed=1200000, transcendentals=0),
     )(got, gain)

time: 143 us -> 143 us (level)
  no operation moved by 1% of the time
where the time goes in v8:
time: 143 us
  blocking collectives  84.6 us (59%)
  starting transfers between devices  16.9 us (12%)
  between operations  13.6 us (10%)
  Pallas kernels  11 us (8%)
  waiting for transfers between devices  10.6 us (7%)
  local copies, waits for them, and re-layouts  4.54 us (3%)
    all_to_all x1, blocking collectives, per_device(): got = lax.all_to_all(payload, ('xh', 'y', 'core'), 0, 0, tiled=True)  29.1 us
    all_to_all x1, blocking collectives, per_device(): lax.all_to_all(asked, ('z', 'xh'), 0, 0, tiled=True).reshape(TOKENS, 1)  24.1 us
    all_to_all x1, blocking collectives, per_device(): lax.all_to_all(jnp.broadcast_to(part[None], (16, 3, 24)), ('y', 'core'),...  16 us
    all_to_all x1, blocking collectives, per_device(): stats = lax.all_to_all(stats, ('z', 'xh'), 0, 0, tiled=True)  15.3 us
    pallas_call x1, Pallas kernels, local_losses(): pl.pallas_call(loss_kernel, out_shape=jax.ShapeDtypeStruct((8, TOKENS), j...  8.71 us
    all_gather x1, waiting for transfers between devices, per_device(): rows = lax.all_gather(normed, 'z', axis=0, tiled=True)  7.42 us
    ppermute x2, starting transfers between devices, per_device(): far_beside = [lax.ppermute(part, 'core', swap) for part in far]  7.09 us
    ppermute x1, starting transfers between devices, per_device(): beside = lax.ppermute(late, 'core', swap)  4.58 us
  transfers between devices with their start and end apart: 6, of which 3 were waited for; matrix products, arithmetic and copies ran while one was open for 4% of the time, Pallas kernels for 0%

profile of v8, /device:TPU:1, one launch (start us, length us, event | category | flops | bytes accessed | tf_op | source)
XLA Modules:
  0.0 142.7 jit_solution(18396835132243832733)
XLA Ops:
  6.5 0.0 copy-start
  6.5 0.0 all-gather.2.cloned.1.call-start
  6.5 0.9 shard_map.46
  7.4 29.1 %all_to_all.21.got_ref = bf16[32,64,128]{2,1,0:T(8,128)(2,1)S(1)} all-to-all(bf16[32,64,128]{2,1,0:T(8,128)(2,1)S(1)} %get-tuple-element.13), channel_id=1, replica_groups=mesh['xh'=2,'xl'=2,'z'=8,'y'=8,'core'=2] {'xh','y','core'}, dimensions={0} | all-to-all | bytes 1048576 | tf_op jit(solution)/shard_map/all_to_all | solution.py:188
  36.5 1.4 %shard_map.47 = bf16[48,5376]{1,0:T(8,128)(2,1)} custom-call(bf16[32,64,128]{2,1,0:T(8,128)(2,1)S(1)} %all_to_all.21.got_ref, f32[5376]{0:T(1024)S(1)} %get-tuple-element.14.gain_ref), custom_call_target="tpu_custom_call" | custom-call | flops 2000000 | bytes 1200000 | tf_op jit(solution)/shard_map/pallas_call | solution.py:153
  37.9 0.0 all-gather.2.cloned.1.call-update
  38.0 0.0 copy-start.1
  38.0 3.6 %fusion.3 = (bf16[128,5376]{1,0:T(8,128)(2,1)}, bf16[128,5376]{1,0:T(8,128)(2,1)}) fusion(bf16[256,5376]{1,0:T(8,128)(2,1)} %refs_1_), kind=kLoop, calls=%fused_computation.13 | loop fusion | bytes 5505024 | tf_op jit(solution)/shard_map/slice | solution.py:194
  41.6 2.0 %collective-permute-start.1 = (bf16[128,5376]{1,0:T(8,128)(2,1)}, bf16[128,5376]{1,0:T(8,128)(2,1)}, u32[]{:S(2)}, u32[]{:S(2)}) collective-permute-start(bf16[128,5376]{1,0:T(8,128)(2,1)} %get-tuple-element.23), channel_id=1, source_target_pairs={{0,384},{128,0},{256,128},{384,256},{1,385},{129,1},{257,129},{385... | collective-permute-start | bytes 4128776 | tf_op jit(solution)/shard_map/ppermute | solution.py:194
  43.6 3.2 %collective-permute-start = (bf16[128,5376]{1,0:T(8,128)(2,1)}, bf16[128,5376]{1,0:T(8,128)(2,1)}, u32[]{:S(2)}, u32[]{:S(2)}) collective-permute-start(bf16[128,5376]{1,0:T(8,128)(2,1)} %get-tuple-element.24), channel_id=1, source_target_pairs={{0,128},{128,256},{256,384},{384,0},{1,129},{129,257},{257,385},{3... | collective-permute-start | bytes 4128776 | tf_op jit(solution)/shard_map/ppermute | solution.py:193
  46.9 0.0 copy-done.1
  46.9 4.6 %collective-permute-start.2 = (bf16[256,5376]{1,0:T(8,128)(2,1)S(1)}, bf16[256,5376]{1,0:T(8,128)(2,1)}, u32[]{:S(2)}, u32[]{:S(2)}) collective-permute-start(bf16[256,5376]{1,0:T(8,128)(2,1)S(1)} %copy-done.1), channel_id=1, source_target_pairs={{0,1},{1,0},{2,3},{3,2},{4,5},{5,4},{6,7},{7,6},{8,9},{9,8},{10,11... | collective-permute-start | bytes 8257544 | tf_op jit(solution)/shard_map/ppermute | solution.py:195
  51.5 0.0 copy-done
  51.5 24.1 %all_to_all.22 = s32[16,1,24]{2,1,0:T(1,128)S(1)} all-to-all(s32[16,1,24]{2,1,0:T(1,128)S(1)} %broadcast_in_dim.4), channel_id=1, replica_groups=mesh['xh'=2,'xl'=2,'z'=8,'y'=8,'core'=2] {'z','xh'}, dimensions={0} | all-to-all | bytes 3072 | tf_op jit(solution)/shard_map/all_to_all | solution.py:197
  75.6 0.5 broadcast.13
  76.1 0.7 reduce.7
  76.8 0.1 reshape.19
  76.9 0.0 collective-permute-done.1.refs_3_
  76.9 0.0 collective-permute-done.refs_2_
  76.9 5.2 %collective-permute-start.3 = (bf16[128,5376]{1,0:T(8,128)(2,1)}, bf16[128,5376]{1,0:T(8,128)(2,1)}, u32[]{:S(2)}, u32[]{:S(2)}) collective-permute-start(bf16[128,5376]{1,0:T(8,128)(2,1)} %collective-permute-done.refs_2_), channel_id=1, source_target_pairs={{0,1},{1,0},{2,3},{3,2},{4,5},{5,4},{6,7},{7,6},{8,9},{9,8},{10,11... | collective-permute-start | bytes 4128776 | tf_op jit(solution)/shard_map/ppermute | solution.py:200
  82.1 1.9 %collective-permute-start.4 = (bf16[128,5376]{1,0:T(8,128)(2,1)}, bf16[128,5376]{1,0:T(8,128)(2,1)}, u32[]{:S(2)}, u32[]{:S(2)}) collective-permute-start(bf16[128,5376]{1,0:T(8,128)(2,1)} %collective-permute-done.1.refs_3_), channel_id=1, source_target_pairs={{0,1},{1,0},{2,3},{3,2},{4,5},{5,4},{6,7},{7,6},{8,9},{9,8},{10,11... | collective-permute-start | bytes 4128776 | tf_op jit(solution)/shard_map/ppermute | solution.py:200
  84.1 0.1 stack.47.refs_8_
  84.2 0.1 copy.23.refs_7_
  84.3 0.9 collective-permute-done.3.refs_5_
  85.2 2.3 %collective-permute-done.4.refs_6_ = bf16[128,5376]{1,0:T(8,128)(2,1)} collective-permute-done((bf16[128,5376]{1,0:T(8,128)(2,1)}, bf16[128,5376]{1,0:T(8,128)(2,1)}, u32[]{:S(2)}, u32[]{:S(2)}) %collective-permute-start.4) | collective-permute-done | bytes 1376288 | tf_op jit(solution)/shard_map/ppermute | solution.py:200
  87.5 0.0 collective-permute-done.2.refs_4_
  87.5 7.4 %all-gather.2.cloned.1.call-done.refs_0_ = bf16[384,5376]{1,0:T(8,128)(2,1)} async-done(((bf16[48,5376]{1,0:T(8,128)(2,1)}), bf16[384,5376]{1,0:T(8,128)(2,1)}) %all-gather.2.cloned.1.call-update) | async-done | bytes 4128784 | tf_op jit(solution)/shard_map/all_gather | solution.py:191
  94.9 8.7 %shard_map.48 = f32[8,384]{1,0:T(8,128)S(1)} custom-call(bf16[384,5376]{1,0:T(8,128)(2,1)} %all-gather.2.cloned.1.call-done.refs_0_, bf16[256,5376]{1,0:T(8,128)(2,1)S(1)} %copy-done.1, bf16[128,5376]{1,0:T(8,128)(2,1)} %collective-permute-done.refs_2_, bf16[128,5376]{1,0:T(8,128)(2,1)} %collective-permute-done.1.refs_3_, ...), custom_call_target="tpu_custom_call" | custom-call | flops 4227858432 | bytes 16777216 | tf_op jit(solution)/shard_map/pallas_call | solution.py:72
  103.6 0.1 reshape.20
  103.7 15.3 %all_to_all.23 = f32[16,3,24]{2,1,0:T(4,128)S(1)} all-to-all(f32[16,3,24]{2,1,0:T(4,128)S(1)} %bitcast.35), channel_id=1, replica_groups=mesh['xh'=2,'xl'=2,'z'=8,'y'=8,'core'=2] {'z','xh'}, dimensions={0} | all-to-all | bytes 9216 | tf_op jit(solution)/shard_map/all_to_all | solution.py:203
  119.1 16.0 %all_to_all.24 = f32[16,3,24]{2,1,0:T(4,128)S(1)} all-to-all(f32[16,3,24]{2,1,0:T(4,128)S(1)} %broadcast_in_dim.5), channel_id=1, replica_groups=mesh['xh'=2,'xl'=2,'z'=8,'y'=8,'core'=2] {'y','core'}, dimensions={0} | all-to-all | bytes 9216 | tf_op jit(solution)/shard_map/all_to_all | solution.py:205
  135.2 0.6 add_subtract_fusion
  (12 shorter events, 0.2 us)
Async XLA Ops:
  6.5 44.9 %copy-start = (s32[2,24]{1,0:T(2,128)S(1)}, s32[2,24]{1,0:T(2,128)}, u32[]{:S(2)}) copy-start(s32[2,24]{1,0:T(2,128)} %param.7) | copy-start | bytes 580
  6.5 88.3 %all-gather.2.cloned.1.call-start = ((), (), s32[]{:S(2)}) async-start(), calls=%async_computation.4 | async-start | bytes 4644864 | tf_op jit(solution)/shard_map/all_gather | solution.py:191
  38.0 8.9 %copy-start.1 = (bf16[256,5376]{1,0:T(8,128)(2,1)S(1)}, bf16[256,5376]{1,0:T(8,128)(2,1)}, u32[]{:S(2)}) copy-start(bf16[256,5376]{1,0:T(8,128)(2,1)} %refs_1_) | copy-start | bytes 8257540
  41.6 35.3 %collective-permute-start.1 = (bf16[128,5376]{1,0:T(8,128)(2,1)}, bf16[128,5376]{1,0:T(8,128)(2,1)}, u32[]{:S(2)}, u32[]{:S(2)}) collective-permute-start(bf16[128,5376]{1,0:T(8,128)(2,1)} %get-tuple-element.23), channel_id=1, source_target_pairs={{0,384},{128,0},{256,128},{384,256},{1,385},{129,1},{257,129},{385... | collective-permute-start | bytes 4128776 | tf_op jit(solution)/shard_map/ppermute | solution.py:194
  43.6 33.3 %collective-permute-start = (bf16[128,5376]{1,0:T(8,128)(2,1)}, bf16[128,5376]{1,0:T(8,128)(2,1)}, u32[]{:S(2)}, u32[]{:S(2)}) collective-permute-start(bf16[128,5376]{1,0:T(8,128)(2,1)} %get-tuple-element.24), channel_id=1, source_target_pairs={{0,128},{128,256},{256,384},{384,0},{1,129},{129,257},{257,385},{3... | collective-permute-start | bytes 4128776 | tf_op jit(solution)/shard_map/ppermute | solution.py:193
  46.9 40.6 %collective-permute-start.2 = (bf16[256,5376]{1,0:T(8,128)(2,1)S(1)}, bf16[256,5376]{1,0:T(8,128)(2,1)}, u32[]{:S(2)}, u32[]{:S(2)}) collective-permute-start(bf16[256,5376]{1,0:T(8,128)(2,1)S(1)} %copy-done.1), channel_id=1, source_target_pairs={{0,1},{1,0},{2,3},{3,2},{4,5},{5,4},{6,7},{7,6},{8,9},{9,8},{10,11... | collective-permute-start | bytes 8257544 | tf_op jit(solution)/shard_map/ppermute | solution.py:195
  76.9 8.3 %collective-permute-start.3 = (bf16[128,5376]{1,0:T(8,128)(2,1)}, bf16[128,5376]{1,0:T(8,128)(2,1)}, u32[]{:S(2)}, u32[]{:S(2)}) collective-permute-start(bf16[128,5376]{1,0:T(8,128)(2,1)} %collective-permute-done.refs_2_), channel_id=1, source_target_pairs={{0,1},{1,0},{2,3},{3,2},{4,5},{5,4},{6,7},{7,6},{8,9},{9,8},{10,11... | collective-permute-start | bytes 4128776 | tf_op jit(solution)/shard_map/ppermute | solution.py:200
  82.1 5.4 %collective-permute-start.4 = (bf16[128,5376]{1,0:T(8,128)(2,1)}, bf16[128,5376]{1,0:T(8,128)(2,1)}, u32[]{:S(2)}, u32[]{:S(2)}) collective-permute-start(bf16[128,5376]{1,0:T(8,128)(2,1)} %collective-permute-done.1.refs_3_), channel_id=1, source_target_pairs={{0,1},{1,0},{2,3},{3,2},{4,5},{5,4},{6,7},{7,6},{8,9},{9,8},{10,11... | collective-permute-start | bytes 4128776 | tf_op jit(solution)/shard_map/ppermute | solution.py:200
Sparse Core Ops, SparseCore 0:
  38.1 56.7 all-gather.1
